TPU v7x, 32 devices: a whole 2x2x4 slice. The times are simulated.
32 devices in a mesh: section: 4 (over y, core), dp: 8 (over z, x).
Axes of the slice: x: 2, y: 2, z: 4, core: 2. Of those that a mesh axis runs over, the one named last changes fastest.
Arguments:
- embeds: bfloat16 [64, 197, 768], P('dp'), may hold values from -6 to 6
- mask: int32 [64, 197], P('dp'), may hold values from 0 to 1, as said below
- cotangent: bfloat16 [64, 197, 768], P('dp'), may hold values from -6 to 6
- section_weight: bfloat16 [4, 768, 3072], P('section')
- down_weight: bfloat16 [4, 3072, 768], P('section'), may hold values from -0.109375 to 0.109375
- section_vectors: float32 [4, 8, 768], P('section')
- rel_table: float32 [4, 12, 732], P('section'), may hold values from -4 to 4
Outputs:
- activations: bfloat16 [4, 64, 197, 768], P('section', 'dp')
- input_grads: float32 [4, 64, 197, 768], P('section', 'dp')
- grad_weight: float32 [4, 768, 3072], P('section')
- grad_down: float32 [4, 3072, 768], P('section')
- grad_vectors: float32 [4, 8, 768], P('section')
- grad_table: float32 [4, 12, 732], P('section')
Inputs may be any that keep to these rules, and one draw needn't show every extreme that they name: `mask`: column 0 (class row) is 0. Each image masks between 40 and 110 of its patches as one compact block around a centre; some image masks exactly 110 and another exactly 40.
All inputs are finite; a program needn't handle non-finite values.
Results may differ from a plain program's by a relative error of at most 0.015.
Values may be sent and summed in bfloat16 or wider, within the bound.
No kernel may reach another device: no remote copies, remote signals or barrier semaphores. Data moves between devices by JAX's collectives and lax.ppermute only.
A program may use at most 192 MiB of HBM per device.

v0:
```python
import math
from functools import partial

import jax
import jax.numpy as jnp
from jax import lax
from jax.experimental import pallas as pl
from jax.experimental.pallas import tpu as pltpu
from jax.sharding import PartitionSpec as P

EPS = 1e-06
F32 = jnp.float32
BF = jnp.bfloat16
HD = 64
RING = 8
ANY = pl.BlockSpec(memory_space=pl.ANY)
VMEM = pl.BlockSpec(memory_space=pltpu.VMEM)
SMEM = pl.BlockSpec(memory_space=pltpu.SMEM)


def dot(left, right):
    return jnp.dot(left, right, preferred_element_type=F32)


def dot_nt(left, right):
    return lax.dot_general(left, right, (((1,), (1,)), ((), ())), preferred_element_type=F32)


def dot_tn(left, right):
    return lax.dot_general(left, right, (((0,), (0,)), ((), ())), preferred_element_type=F32)


def norm_stats(x):
    center = x - jnp.mean(x, -1, keepdims=True)
    rstd = lax.rsqrt(jnp.mean(center * center, -1, keepdims=True) + EPS)
    return center * rstd, rstd


def norm_back(g, da, xhat, rstd, gain):
    w = da * gain
    return g + rstd * (w - jnp.mean(w, -1, keepdims=True) - xhat * jnp.mean(w * xhat, -1, keepdims=True))


def rows_sum(v):
    return jnp.sum(v, 0, keepdims=True)


def gelu_parts(h):
    z = jnp.abs(h) * 0.7071067811865476
    t = 1.0 / (1.0 + 0.3275911 * z)
    gauss = jnp.exp(-0.5 * h * h)
    poly = t * (0.127414796 + t * (-0.142248368 + t * (0.7107068705 + t * (-0.7265760135 + t * 0.5307027145))))
    tail = poly * gauss
    phi = jnp.where(h >= 0.0, 1.0 - tail, tail)
    return h * phi, phi + h * (gauss * 0.3989422804014327)


class Copies:
    def __init__(self, sems):
        self.sems, self.used, self.out = sems, 0, []

    def start(self, src, dst):
        copy = pltpu.make_async_copy(src, dst, self.sems.at[self.used])
        self.used += 1
        copy.start()
        return copy

    def choose(self, first, a, b, dst):
        sem = self.sems.at[self.used]
        self.used += 1

        @pl.when(first)
        def _():
            pltpu.make_async_copy(a, dst, sem).start()

        @pl.when(jnp.logical_not(first))
        def _():
            pltpu.make_async_copy(b, dst, sem).start()

        return pltpu.make_async_copy(a, dst, sem)

    def store(self, src, dst):
        self.out.append(self.start(src, dst))

    def finish(self):
        for copy in self.out:
            copy.wait()


def image_of(ref, i):
    return ref.at[i] if len(ref.shape) == 3 else ref


def head_masks(scale):
    lane = lax.broadcasted_iota(jnp.int32, (1, 2 * HD), 1)
    low = jnp.where(lane < HD, scale, 0.0).astype(BF)
    high = jnp.where(lane < HD, 0.0, scale).astype(BF)
    return low, high


def forward_image(i, refs_in, refs_state, refs_extra, scratch):
    flags, x_ref, vec_ref, vecf_ref, wa_ref, w1_ref, w2_ref, bias_ref = refs_in
    x_ref = image_of(x_ref, i)
    sa, a1, ctx, y1, pb, g_all, a2, gp, b2, y2 = refs_state
    (send,) = refs_extra
    x_v, qkv_v, pb_v, b_v, y_v, gp_v, bf_v, yf_v, sems = scratch
    rows, width = x_v.shape
    heads, keys = pb_v.shape[0], pb_v.shape[2]
    hidden = gp_v.shape[1]
    a_v, c_v, g_v, af_v = a1.at[i], ctx.at[i], g_all.at[i], a2.at[i]

    @pl.when(flags[0] == 1)
    def _():
        cp = Copies(sems)
        x_v[...] = x_ref[...]
        cp.store(x_v, sa.at[i, 0])
        xhat, rstd = norm_stats(x_v[...].astype(F32))
        a_v[...] = (xhat * vec_ref[0:1, :] + vec_ref[1:2, :]).astype(BF)
        qkv_v[rows:, :] = jnp.zeros((keys - rows, 3 * width), BF)
        a = a_v[...]
        block = 256
        for j in range(3 * width // block):
            cols = slice(j * block, (j + 1) * block)
            part = dot(a, wa_ref[:, cols])
            kind, at = divmod(j * block, width)
            if kind == 0:
                part = part + vec_ref[4:5, at : at + block]
            if kind == 2:
                part = part + vec_ref[5:6, at : at + block]
            qkv_v[0:rows, cols] = part.astype(BF)
        for kind in range(3):
            cp.store(qkv_v.at[0:rows, pl.ds(kind * width, width)], sa.at[i, 1 + kind])
        scaled = head_masks(HD ** (-0.5))
        plain = head_masks(1.0)
        for j in range(heads // 2):
            q = qkv_v[0:rows, j * 128 : (j + 1) * 128]
            k = qkv_v[:, width + j * 128 : width + (j + 1) * 128]
            u = qkv_v[:, 2 * width + j * 128 : 2 * width + (j + 1) * 128]
            total = None
            for t in range(2):
                s = dot_nt(q * scaled[t], k) + bias_ref[2 * j + t]
                e = jnp.exp(s - jnp.max(s, -1, keepdims=True))
                p = (e * (1.0 / jnp.sum(e, -1, keepdims=True))).astype(BF)
                pb_v[2 * j + t] = p
                part = dot(p, u * plain[t])
                total = part if total is None else total + part
            c_v[:, j * 128 : (j + 1) * 128] = total.astype(BF)
        cp.store(pb_v, pb.at[i])
        b = dot(c_v[...], wa_ref[:, 3 * width :]) + vec_ref[3:4, :]
        b_v[...] = b.astype(BF)
        cp.store(b_v, sa.at[i, 4])
        y_v[...] = (x_v[...].astype(F32) + vec_ref[2:3, :] * b).astype(BF)
        cp.store(y_v, y1.at[i])

        xhat, rstd = norm_stats(y_v[...].astype(F32))
        af_v[...] = (xhat * vecf_ref[0:1, :] + vecf_ref[1:2, :]).astype(BF)
        a = af_v[...]
        for j in range(hidden // block):
            row, at = divmod(j * block, width)
            cols = slice(j * block, (j + 1) * block)
            h = dot(a, w1_ref[:, cols]) + vecf_ref[4 + row : 5 + row, at : at + block]
            value, slope = gelu_parts(h)
            g_v[:, cols] = value.astype(BF)
            gp_v[:, cols] = slope.astype(BF)
        cp.store(gp_v, gp.at[i])
        b = dot(g_v[...], w2_ref[...]) + vecf_ref[3:4, :]
        yf_v[...] = (y_v[...].astype(F32) + vecf_ref[2:3, :] * b).astype(BF)
        send[...] = yf_v[...]
        cp.store(yf_v, y2.at[i])
        bf_v[...] = b.astype(BF)
        cp.store(bf_v, b2.at[i])
        cp.finish()


def backward_image(i, refs_in, refs_state, refs_extra, scratch):
    flags, g_ref, vec_ref, vecf_ref, wa_ref, w1_ref, w2_ref, sa, pb, y1, gp, b2 = refs_in
    g_ref = image_of(g_ref, i)
    dh_all, ef, dx1, vgf, ea, dq, dl, dx0, vga = refs_state
    (send,) = refs_extra
    (gin_v, gp_v, bf_v, xf_v, qkv_v, pb_v, b_v, x_v, dx_v, vgf_v, dc_v, dl_v, dx0_v, vg_v, sems) = scratch
    e_v, dh_v, ea_v, dq_v = ef.at[i], dh_all.at[i], ea.at[i], dq.at[i]
    rows, width = x_v.shape
    heads, keys = pb_v.shape[0], pb_v.shape[2]
    hidden = dh_v.shape[1]

    @pl.when(flags[0] == 1)
    def _():
        cp = Copies(sems)
        in_gp = cp.start(gp.at[i], gp_v)
        in_bf = cp.start(b2.at[i], bf_v)
        in_xf = cp.start(y1.at[i], xf_v)
        ins = [cp.start(sa.at[i, 1 + kind], qkv_v.at[0:rows, pl.ds(kind * width, width)]) for kind in range(3)]
        in_pb = cp.start(pb.at[i], pb_v)
        in_b = cp.start(sa.at[i, 4], b_v)
        in_x = cp.start(sa.at[i, 0], x_v)
        qkv_v[rows:, :] = jnp.zeros((keys - rows, 3 * width), BF)
        vg_v[6:8, :] = jnp.zeros((2, width), F32)
        gin_v[...] = g_ref[...]
        scaled = gin_v[...].astype(F32) * vecf_ref[2:3, :]
        e_v[...] = scaled.astype(BF)
        vgf_v[3:4, :] = rows_sum(scaled)
        in_gp.wait()
        e = e_v[...]
        block = 256
        for j in range(hidden // block):
            row, at = divmod(j * block, width)
            cols = slice(j * block, (j + 1) * block)
            dh = dot_nt(e, w2_ref[cols, :]) * gp_v[:, cols].astype(F32)
            dh_v[:, cols] = dh.astype(BF)
            vgf_v[4 + row : 5 + row, at : at + block] = rows_sum(dh)
        in_bf.wait()
        in_xf.wait()
        vgf_v[2:3, :] = rows_sum(gin_v[...].astype(F32) * bf_v[...].astype(F32))
        da = dot_nt(dh_v[...], w1_ref[...])
        xhat, rstd = norm_stats(xf_v[...].astype(F32))
        vgf_v[0:1, :] = rows_sum(da * xhat)
        vgf_v[1:2, :] = rows_sum(da)
        cp.store(vgf_v, vgf.at[i])
        dx_v[...] = norm_back(gin_v[...].astype(F32), da, xhat, rstd, vecf_ref[0:1, :]).astype(BF)
        cp.store(dx_v, dx1.at[i])

        scaled = dx_v[...].astype(F32) * vec_ref[2:3, :]
        ea_v[...] = scaled.astype(BF)
        vg_v[3:4, :] = rows_sum(scaled)
        dc_v[...] = dot_nt(ea_v[...], wa_ref[:, 3 * width :]).astype(BF)
        for copy in ins:
            copy.wait()
        in_pb.wait()
        factor = HD ** (-0.5)
        plain = head_masks(1.0)
        for j in range(heads // 2):
            cols = slice(j * 128, (j + 1) * 128)
            q = qkv_v[0:rows, j * 128 : (j + 1) * 128]
            k = qkv_v[:, width + j * 128 : width + (j + 1) * 128]
            u = qkv_v[:, 2 * width + j * 128 : 2 * width + (j + 1) * 128]
            dc = dc_v[:, cols]
            dq_t, dk_t, du_t = None, None, None
            for t in range(2):
                dc_t = dc * plain[t]
                p = pb_v[2 * j + t]
                dp = dot_nt(dc_t, u)
                pf = p.astype(F32)
                wp = pf * dp
                ds = wp - pf * jnp.sum(wp, -1, keepdims=True)
                dlog = (ds * factor).astype(BF)
                dl_v[2 * j + t] = dlog
                du = dot_tn(p, dc_t)
                dqp = dot(dlog, k * plain[t])
                dkp = dot_tn(dlog, q * plain[t])
                dq_t = dqp if dq_t is None else dq_t + dqp
                dk_t = dkp if dk_t is None else dk_t + dkp
                du_t = du if du_t is None else du_t + du
            dq_v[:, j * 128 : (j + 1) * 128] = dq_t.astype(BF)
            dq_v[:, width + j * 128 : width + (j + 1) * 128] = dk_t[0:rows].astype(BF)
            dq_v[:, 2 * width + j * 128 : 2 * width + (j + 1) * 128] = du_t[0:rows].astype(BF)
            vg_v[4:5, cols] = rows_sum(dq_t)
            vg_v[5:6, cols] = rows_sum(du_t)
        cp.store(dl_v, dl.at[i])
        in_b.wait()
        in_x.wait()
        vg_v[2:3, :] = rows_sum(dx_v[...].astype(F32) * b_v[...].astype(F32))
        da = dot_nt(dq_v[...], wa_ref[:, 0 : 3 * width])
        xhat, rstd = norm_stats(x_v[...].astype(F32))
        dx0_v[...] = norm_back(dx_v[...].astype(F32), da, xhat, rstd, vec_ref[0:1, :]).astype(BF)
        send[...] = dx0_v[...]
        cp.store(dx0_v, dx0.at[i])
        vg_v[0:1, :] = rows_sum(da * xhat)
        vg_v[1:2, :] = rows_sum(da)
        cp.store(vg_v, vga.at[i])
        cp.finish()


def load_weights(refs_in, refs_out, scratch):
    flags, own_ref, other_ref, own_d, other_d = refs_in
    wa_ref, w1_ref, w2_ref = refs_out
    first = flags[1] == 0
    cp = Copies(scratch[0])
    for copy in (
        cp.choose(first, own_ref, other_ref, wa_ref),
        cp.choose(first, other_ref, own_ref, w1_ref),
        cp.choose(first, other_d, own_d, w2_ref),
    ):
        copy.wait()


def weight_parts(ups, refs_in, sents, owns, scratch):
    flags, g_all, dh_all, a2, ef, a1, ctx, dq, ea = refs_in
    sent_v, own_v, sems = scratch
    width = a2.shape[2]
    chunks, tall = own_v.shape[1], a2.shape[2] // own_v.shape[1]
    part = tall // 2
    cp = Copies(sems)
    core, at = flags[0], flags[1]
    low = core == 0
    cuts = 2
    block, group = width // cuts, chunks // cuts
    rows = a2.shape[0] * a2.shape[1]

    def product(left, right, first_col, second_col, put):
        rhs = right[:, :, second_col : second_col + width].reshape(rows, width)

        def one(k, none):
            start = pl.multiple_of(first_col + k * block, 128)
            lhs = left[:, :, pl.ds(start, block)].reshape(rows, block)
            put(pl.ds(k * group, group), dot_tn(lhs, rhs).astype(BF).reshape(group, tall, width))
            return none

        lax.fori_loop(0, cuts, one, 0)

    def share(turn, s, which, target):
        def put(group, value):
            target[turn % 2, group, 0:tall] = value

        @pl.when(core == which)
        def _():
            product(a2, dh_all, 0, s * width, put)

        @pl.when(core != which)
        def _():
            product(g_all, ef, s * width, 0, put)

    def put_both(turn, group, value):
        sent_v[turn % 2, group, tall:] = jnp.where(low, value[:, part:], value[:, :part])
        own_v[turn % 2, group, tall:] = jnp.where(low, value[:, :part], value[:, part:])

    def store(turn, s, source, target):
        for chunk in range(chunks):
            slot = (at - chunk if ups[s] else chunk - at) & (chunks - 1)
            cp.store(source.at[turn % 2, chunk], target.at[slot])

    for turn, s in enumerate((0, 2, 1, 3)):
        if turn >= 2:
            for copy in cp.out[: 2 * chunks]:
                copy.wait()
            cp.out = cp.out[2 * chunks :]
        if s < 3:
            product(a1, dq, 0, s * width, partial(put_both, turn))
        else:
            product(ctx, ea, 0, 0, partial(put_both, turn))
        share(turn, s, 1, sent_v)
        store(turn, s, sent_v, sents[s])
        share(turn, s, 0, own_v)
        store(turn, s, own_v, owns[s])
    cp.finish()


def table_fold(grid, dl, by_col, edge, dl_v, sems):
    images, heads, rows, keys = dl.shape
    patches = grid * grid
    wide = by_col.shape[2]
    copies = []
    for h in range(heads):
        copy = pltpu.make_async_copy(dl.at[:, h], dl_v.at[h], sems.at[h])
        copy.start()
        copies.append(copy)
    lane = lax.broadcasted_iota(jnp.int32, (1, keys), 1)
    inner = lane > 0
    for h in range(heads):
        copies[h].wait()
        total = dl_v[h, 0].astype(F32)
        for i in range(1, images):
            total = total + dl_v[h, i].astype(F32)
        edge[h, 0:1, :] = total[0:1]
        edge[h, 1:2, :] = jnp.broadcast_to(jnp.sum(total[1 : 1 + patches, 0:1], 0, keepdims=True), (1, keys))
        block = jnp.where(inner, total, 0.0)
        sums = None
        for r in range(grid):
            part = block[1 + r * grid : 1 + (r + 1) * grid]
            part = jnp.concatenate([part, jnp.zeros((grid, wide - keys), F32)], 1)
            part = pltpu.roll(part, (grid * (grid - 1 - r) - 1) % wide, 1)
            sums = part if sums is None else sums + part
        by_col[h] = sums


def place_sums(refs_in, refs_out, scratch):
    flags, a_up, a_down, b_up, b_down = refs_in
    gw, gd = refs_out
    gw_v, gd_v, sems = scratch
    blocks, tall, width = gd_v.shape
    low = flags[0] == 0
    cp = Copies(sems)
    for way, (a_ref, b_ref) in enumerate(((a_up, b_up), (a_down, b_down))):
        chunk = flags[1 + way]
        row = pl.multiple_of(chunk * tall, tall)
        for k in range(blocks // 2):
            s = way * (blocks // 2) + k
            a = a_ref[k].astype(F32)
            gw_v[s] = jnp.where(low, a, b_ref[k].astype(F32))
            gd_v[s] = jnp.where(low, 0.0, a)
            cp.store(gw_v.at[s], gw.at[pl.ds(row, tall), pl.ds(s * width, width)])
            cp.store(gd_v.at[s], gd.at[pl.ds(pl.multiple_of(s * width + row, tall), tall)])
    cp.finish()


def bias_fill(grid, tail, by_col, out):
    heads, rows, keys = out.shape
    patches = grid * grid
    wide = by_col.shape[2]
    lane = lax.broadcasted_iota(jnp.int32, (1, keys), 1)
    for h in range(heads):
        corner, upper, left = tail[h, 2], tail[h, 0], tail[h, 1]
        out[h, patches + 1 :, :] = jnp.where(
            lax.broadcasted_iota(jnp.int32, (rows - patches - 1, keys), 1) <= patches, 0.0, -1e30
        )
        out[h, 0:1, :] = jnp.where(lane == 0, corner, jnp.where(lane <= patches, upper, -1e30))
        block = by_col[h]
        for r in range(grid):
            turned = pltpu.roll(block, (1 - grid * (grid - 1 - r)) % wide, 1)[0:grid, 0:keys]
            turned = jnp.where(lane == 0, left, jnp.where(lane <= patches, turned, -1e30))
            out[h, 1 + r * grid : 1 + (r + 1) * grid, :] = turned


def run(body, i, name, ins, specs, state, shapes, extra, scratch, sems, flops, moved):
    fresh = state is None
    ins = [in_hbm(v) if spec is ANY else v for v, spec in zip(ins, specs)]
    n_in, n_state, n_extra = len(ins), len(shapes), len(extra)
    given = 0 if fresh else n_state

    def kernel(*refs):
        refs_in = refs[:n_in]
        outs = refs[n_in + given : n_in + given + n_state]
        more = refs[n_in + given + n_state : n_in + given + n_state + n_extra]
        body(i, refs_in, outs, more, refs[n_in + given + n_state + n_extra :])

    made = pl.pallas_call(
        kernel,
        out_shape=tuple(shapes) + tuple(extra),
        in_specs=list(specs) + [ANY] * given,
        out_specs=tuple(VMEM if in_vmem(v) else ANY for v in [*shapes, *extra]),
        scratch_shapes=[pltpu.VMEM(s.shape, s.dtype) for s in scratch] + [pltpu.SemaphoreType.DMA((sems,))],
        input_output_aliases={} if fresh else {n_in + k: k for k in range(n_state)},
        compiler_params=pltpu.CompilerParams(vmem_limit_bytes=16 * 2**20),
        cost_estimate=pl.CostEstimate(flops=flops, bytes_accessed=moved, transcendentals=0),
        name=name,
    )(*ins, *([] if fresh else state))
    return list(made[:n_state]), list(made[n_state:])


def in_vmem(shape):
    return shape.memory_space == pltpu.VMEM


def pinned(block):
    return pltpu.with_memory_space_constraint(block, pltpu.VMEM)


def in_hbm(block):
    return pltpu.with_memory_space_constraint(block, pltpu.HBM)


def far(shape, dtype=BF):
    return pltpu.HBM(shape, dtype)


def sd(shape, dtype=BF):
    return jax.ShapeDtypeStruct(shape, dtype)


class Kernels:
    def __init__(self, images, rows, keys, width, hidden, heads):
        self.n, self.r, self.k, self.d, self.f, self.h = images, rows, keys, width, hidden, heads

    def weights(self, flags, own, other, own_d, other_d):
        d, f = self.d, self.f
        return pl.pallas_call(
            lambda *refs: load_weights(refs[:5], refs[5:8], refs[8:]),
            out_shape=(pltpu.VMEM((d, f), BF), pltpu.VMEM((d, f), BF), pltpu.VMEM((f, d), BF)),
            in_specs=[SMEM] + [ANY] * 4,
            out_specs=(VMEM, VMEM, VMEM),
            scratch_shapes=[pltpu.SemaphoreType.DMA((3,))],
            compiler_params=pltpu.CompilerParams(vmem_limit_bytes=4 * 2**20),
            name="load_weights",
        )(flags, *[in_hbm(v) for v in (own, other, own_d, other_d)])

    def forward(self, i, flags, x, vec_a, vec_f, weights, bias, state):
        n, r, k, d, f, h = self.n, self.r, self.k, self.d, self.f, self.h
        narrow, wide = far((n, r, d)), far((n, r, f))
        held = pltpu.VMEM((n, r, d), BF)
        shapes = [far((n, 5, r, d)), held, held, narrow, far((n, h, r, k)), pltpu.VMEM((n, r, f), BF), held, wide, narrow, narrow]
        row, high = sd((r, d)), sd((r, f))
        scratch = [row, sd((k, 3 * d)), sd((h, r, k)), row, row, high, row, row]
        ins = [flags, pinned(x), vec_a, vec_f, *[pinned(w) for w in weights], pinned(bias)]
        flops = 2 * r * d * 4 * d + 4 * h * r * k * HD + 4 * r * d * f
        return run(forward_image, i, "forward_image", ins, [SMEM] + [VMEM] * 7, state, shapes, [pltpu.VMEM((r, d), BF)], scratch, 20, flops, 12000000)

    def backward(self, i, flags, g, vec_a, vec_f, weights, kept, state):
        n, r, k, d, f, h = self.n, self.r, self.k, self.d, self.f, self.h
        narrow = far((n, r, d))
        sums = far((n, 8, d), F32)
        held = pltpu.VMEM((n, r, d), BF)
        shapes = [pltpu.VMEM((n, r, f), BF), held, narrow, sums, held, pltpu.VMEM((n, r, 3 * d), BF), far((n, h, r, k)), narrow, sums]
        row, high, pairs, vec = sd((r, d)), sd((r, f)), sd((h, r, k)), sd((8, d), F32)
        scratch = [row, high, row, row, sd((k, 3 * d)), pairs, row, row, row, vec, row, pairs, row, vec]
        sa, a1, ctx, y1, pb, g_all, a2, gp, b2, y2 = kept
        ins = [flags, pinned(g), vec_a, vec_f, *[pinned(w) for w in weights], sa, pb, y1, gp, b2]
        flops = 2 * r * d * 4 * d + 8 * h * r * k * HD + 4 * r * d * f
        return run(backward_image, i, "backward_image", ins, [SMEM] + [VMEM] * 6 + [ANY] * 5, state, shapes, [pltpu.VMEM((r, d), BF)], scratch, 24, flops, 12000000)

    def parts(self, ups, flags, blocks, chunks):
        d = self.d
        tall = d // chunks
        both = (chunks, tall + tall // 2, d)
        made = pl.pallas_call(
            lambda *refs: weight_parts(ups, refs[:9], refs[9:13], refs[13:17], refs[17:]),
            out_shape=(far(both),) * 8,
            in_specs=[SMEM] + [VMEM] * 8,
            out_specs=(ANY,) * 8,
            scratch_shapes=[pltpu.VMEM((2, *both), BF)] * 2 + [pltpu.SemaphoreType.DMA((8 * chunks,))],
            compiler_params=pltpu.CompilerParams(vmem_limit_bytes=28 * 2**20),
            cost_estimate=pl.CostEstimate(flops=1, bytes_accessed=1, transcendentals=0),
            name="weight_parts",
        )(flags, *[pinned(v) for v in blocks])
        return made[:4], made[4:]

    def table(self, dl, grid):
        n, heads, rows, keys = dl.shape
        side = 2 * grid - 1
        wide = -(-(side * grid) // 128) * 128
        by_col, edge = pl.pallas_call(
            partial(table_fold, grid),
            out_shape=(sd((heads, grid, wide), F32), sd((heads, 2, keys), F32)),
            in_specs=[ANY],
            out_specs=(VMEM, VMEM),
            scratch_shapes=[pltpu.VMEM((heads, n, rows, keys), BF), pltpu.SemaphoreType.DMA((heads,))],
            compiler_params=pltpu.CompilerParams(vmem_limit_bytes=24 * 2**20),
            name="table_fold",
        )(in_hbm(dl))
        by_col = by_col[:, :, : side * grid].reshape(heads, grid, side, grid)
        flipped = 0.0
        for c in range(grid):
            at = grid - 1 - c
            flipped = flipped + jnp.pad(by_col[:, c], ((0, 0), (0, 0), (at, side - at - grid)))
        inner = flipped[:, ::-1, ::-1].reshape(heads, side * side)
        patches = grid * grid
        tail = jnp.stack([jnp.sum(edge[:, 0, 1 : 1 + patches], 1), edge[:, 1, 0], edge[:, 0, 0]], 1)
        return jnp.concatenate([inner, tail], 1)

    def place(self, flags, a_up, a_down, b_up, b_down, state):
        d, f = self.d, self.f
        blocks, tall = 2 * a_up.shape[0], a_up.shape[1]
        given = 0 if state is None else 2
        scratch = [pltpu.VMEM((blocks, tall, d), F32)] * 2 + [pltpu.SemaphoreType.DMA((2 * blocks,))]
        return pl.pallas_call(
            lambda *refs: place_sums(refs[:5], refs[5 + given : 7 + given], refs[7 + given :]),
            out_shape=(sd((d, f), F32), sd((f, d), F32)),
            in_specs=[SMEM] + [VMEM] * 4 + [ANY] * given,
            out_specs=(ANY, ANY),
            scratch_shapes=scratch,
            input_output_aliases={5: 0, 6: 1} if given else {},
            compiler_params=pltpu.CompilerParams(vmem_limit_bytes=24 * 2**20),
            cost_estimate=pl.CostEstimate(flops=0, bytes_accessed=1, transcendentals=0),
            name="place_sums",
        )(flags, a_up, a_down, b_up, b_down, *(() if state is None else state))

    def bias(self, table, grid):
        heads = table.shape[0]
        side = 2 * grid - 1
        flipped = table[:, : side * side].reshape(heads, side, side)[:, ::-1, ::-1]
        by_col = jnp.stack([flipped[:, :, grid - 1 - c : side - c] for c in range(grid)], 1)
        by_col = by_col.reshape(heads, grid, side * grid)
        wide = -(-(side * grid) // 128) * 128
        by_col = jnp.pad(by_col, ((0, 0), (0, -grid % 8), (0, wide - side * grid)))
        return pl.pallas_call(
            partial(bias_fill, grid),
            out_shape=pltpu.VMEM((heads, self.r, self.k), F32),
            in_specs=[SMEM, VMEM],
            out_specs=VMEM,
            compiler_params=pltpu.CompilerParams(vmem_limit_bytes=24 * 2**20),
            name="bias_fill",
        )(table[:, side * side :], by_col)


def swap(block, pairs):
    return lax.ppermute(block, "section", pairs)


def ring_order(n):
    return list(range(0, n, 2)) + list(range(n - 1, 0, -2))


def doubled_sum(block, axis):
    n = lax.axis_size(axis)
    step = 1
    while step < n:
        block = block + lax.ppermute(block, axis, [(k, k ^ step) for k in range(n)])
        step *= 2
    return block


def weight_shares(kern, blocks, core, both):
    n = lax.axis_size("dp")
    ringed = n == RING
    place = [0] * n
    for k, device in enumerate(ring_order(n)):
        place[device] = k
    at = jnp.array(place, jnp.int32)[lax.axis_index("dp")] if ringed else jnp.int32(0)
    flags = jnp.stack([core, at])
    sents, owns = kern.parts([ringed, ringed, False, False], flags, blocks, RING)
    got = {s: swap(sents[s], both) for s in (0, 2, 1, 3)}
    return [(owns[s], got[s]) for s in range(4)], at


def weight_sums(kern, locals_, at, small, low, core, to_low, to_high, sections):
    axis = "dp"
    n = lax.axis_size(axis)
    ringed = n == RING
    chunks = RING
    order = ring_order(n)
    tall = kern.d // chunks
    if not ringed:
        sums = [lax.psum((own.astype(F32) + got.astype(F32)).astype(BF), axis) for own, got in locals_]
        first = jnp.stack([v[:, :tall] for v in sums])
        second = jnp.stack([v[:, tall:] for v in sums])
        got_first, got_second = swap(first, to_high), swap(second, to_low)
        kept = jnp.concatenate([second, got_second], 2)
        columns = jnp.where(low, kept, got_first).transpose(1, 2, 0, 3)
        grad_weight = columns.reshape(kern.d, kern.f).astype(F32)
        grad_down = jnp.where(low, 0.0, first.astype(F32)).reshape(kern.f, kern.d)
        return grad_weight, grad_down, doubled_sum(small, axis)

    route = {w: [(order[k], order[(k + w) % n]) for k in range(n)] for w in (1, -1)}
    upper = {
        w: [(s * n + p, s * n + q) for s in range(1, sections, 2) for p, q in route[w]] for w in (1, -1)
    }
    held = [None] * 4
    for k in range(n):
        for s in (0, 2, 1, 3):
            own, other = locals_[s]
            total = own[k].astype(F32) + other[k].astype(F32)
            if k > 0:
                total = total + lax.ppermute(held[s], axis, route[1 if s < 2 else -1]).astype(F32)
            held[s] = total.astype(BF)
    first = jnp.stack([v[:tall] for v in held])
    second = jnp.stack([v[tall:] for v in held])
    got_first, got_second = swap(first, to_high), swap(second, to_low)
    kept = jnp.where(low, jnp.concatenate([second, got_second], 1), first)
    a = {1: kept[:2], -1: kept[2:]}
    b = {1: got_first[:2], -1: got_first[2:]}
    state = None
    step, other = 1, None
    for k in range(n):
        index = jnp.stack([core, (at + 1 - k) & (n - 1), (at - 1 + k) & (n - 1)])
        if k < n - 1:
            next_a = {w: lax.ppermute(a[w], axis, route[w]) for w in (1, -1)}
            next_b = {w: lax.ppermute(b[w], ("section", axis), upper[w]) for w in (1, -1)}
        state = kern.place(index, a[1], a[-1], b[1], b[-1], state)
        if k < n - 1:
            if k % 2 == 0 and step < n:
                other = lax.ppermute(small, axis, [(d, d ^ step) for d in range(n)])
                step *= 2
            if k % 2 == 1 and other is not None:
                small, other = small + other, None
            a, b, state, small = lax.optimization_barrier((next_a, next_b, state, small))
    return (*state, small)


def on_device(embeds, mask, cotangent, section_weight, down_weight, section_vectors, rel_table):
    sections = lax.axis_size("section")
    now = lax.axis_index("section")
    core, stage = now % 2, now // 2
    images, length, width = embeds.shape
    half = images // 2
    hidden = section_weight.shape[2]
    heads = rel_table.shape[1]
    rows, keys = -(-length // 16) * 16, -(-length // 128) * 128
    grid = math.isqrt(length - 1)
    both = [(s, s ^ 1) for s in range(sections)]
    to_low = [(s, s - 1) for s in range(1, sections, 2)]
    to_high = [(s, s + 1) for s in range(0, sections, 2)]
    onward = [(s, s + 2) for s in range(sections - 2)]
    back = [(s + 2, s) for s in range(sections - 2)]
    low = core == 0

    own_w, own_d, own_v, own_t = section_weight[0], down_weight[0], section_vectors[0], rel_table[0]
    other_v = swap(own_v, both)
    table = jnp.where(low, own_t, swap(own_t, to_high))
    other_w = swap(own_w, both)
    other_d = swap(own_d, to_low)
    vec_a, vec_f = jnp.where(low, own_v, other_v), jnp.where(low, other_v, own_v)

    def mine_of(block):
        return lax.dynamic_slice_in_dim(block, core * half, half, 0)

    cover = mine_of(mask)[:, :, None] == 1
    start = jnp.where(cover, vec_a[6].astype(BF), mine_of(embeds))
    pad = ((0, 0), (0, rows - length), (0, 0))
    start = jnp.pad(start, pad)
    upstream = jnp.pad(mine_of(cotangent), pad)

    kern = Kernels(half, rows, keys, width, hidden, heads)
    bias = kern.bias(table, grid)
    flags_a = jnp.stack([(stage == 0).astype(jnp.int32), core])
    flags_b = jnp.stack([(stage == 1).astype(jnp.int32), core])
    weights = kern.weights(flags_a, own_w, other_w, own_d, other_d)
    kept, grads = None, None

    def forward(i, flags, x):
        nonlocal kept
        kept, (send,) = kern.forward(i, flags, x, vec_a, vec_f, weights, bias, kept)
        return send

    arrived = [swap(forward(i, flags_a, start), onward) for i in range(half)]
    for i in range(half):
        forward(i, flags_b, arrived[i])

    def backward(i, flags, g):
        nonlocal grads
        grads, (send,) = kern.backward(i, flags, g, vec_a, vec_f, weights, kept, grads)
        return send

    returned = [swap(backward(i, flags_b, upstream), back) for i in range(half)]
    for i in range(half):
        backward(i, flags_a, returned[i])

    sa, a1, ctx, y1, pb, g_all, a2, gp, b2, y2 = kept
    dh_all, ef, dx1, vgf, ea, dq, dl, dx0, vga = grads
    shares, at = weight_shares(kern, (g_all, dh_all, a2, ef, a1, ctx, dq, ea), core, both)
    own_parts, vga, vgf, dl, dx0, dx1 = lax.optimization_barrier(([v[0] for v in shares], vga, vgf, dl, dx0, dx1))
    shares = [(own, other) for own, (_, other) in zip(own_parts, shares)]
    rows_a = jnp.sum(vga, 0)
    token = jnp.sum(jnp.where(cover, dx0[:, :length].astype(F32), 0.0), (0, 1))
    rows_a = rows_a.at[6].add(jnp.where(stage == 0, token, 0.0))
    rows_f = jnp.sum(vgf, 0)
    row_terms = jnp.where(low, rows_a, rows_f) + swap(jnp.where(low, rows_f, rows_a), both)
    sums = kern.table(dl, grid) * (HD ** 0.5)
    sums = jnp.where(low, sums + swap(sums, to_low), 0.0)
    entries = sums.shape[1]
    wide = -(-entries // 128) * 128
    small = jnp.concatenate([row_terms.reshape(-1), jnp.pad(sums, ((0, 0), (0, wide - entries))).reshape(-1)])
    grad_weight, grad_down, small = weight_sums(
        kern,
        shares,
        at,
        small.reshape(-1, 128),
        low, core, to_low, to_high, sections
    )

    small = small.reshape(-1)
    grad_rows = small[: 8 * width].reshape(8, width)
    grad_table = small[8 * width :].reshape(heads, wide)[:, :entries]

    def gather_images(a_part, f_part):
        mine, theirs = jnp.where(low, a_part, f_part), jnp.where(low, f_part, a_part)
        got = swap(theirs, both)
        return jnp.concatenate([jnp.where(low, mine, got), jnp.where(low, got, mine)], 0)[:, :length]

    activations = gather_images(y1, y2)
    input_grads = gather_images(dx0, dx1).astype(F32)
    hide = (mask[:, :, None] == 1) & (now == 0)
    input_grads = jnp.where(hide, 0.0, input_grads)
    return (
        activations[None],
        input_grads[None],
        grad_weight[None],
        grad_down[None],
        grad_rows[None],
        grad_table[None],
    )


def solution(mesh):
    placed = (
        P("dp", None, None),
        P("dp", None),
        P("dp", None, None),
        P("section", None, None),
        P("section", None, None),
        P("section", None, None),
        P("section", None, None),
    )
    return jax.shard_map(
        on_device,
        mesh=mesh,
        in_specs=placed,
        out_specs=(
            P("section", "dp", None, None),
            P("section", "dp", None, None),
            P("section", None, None),
            P("section", None, None),
            P("section", None, None),
            P("section", None, None),
        ),
        check_vma=False,
    )
```

profile of v0, /device:TPU:1, one launch (start us, length us, event | category | flops | bytes accessed | tf_op | source)
XLA Modules:
  0.0 411.0 jit_solution(11611598504497180380)
XLA Ops:
  0.8 4.6 %collective-permute-start.2 = (bf16[3072,768]{1,0:T(8,128)(2,1)}, bf16[3072,768]{1,0:T(8,128)(2,1)}, u32[]{:S(2)}, u32[]{:S(2)}) collective-permute-start(bf16[3072,768]{1,0:T(8,128)(2,1)} %bitcast.226), channel_id=1, source_target_pairs={{8,0},{24,16},{9,1},{25,17},{10,2},{26,18},{11,3},{27,19},{12,4},{... | collective-permute-start | bytes 14155784 | tf_op jit(solution)/shard_map/ppermute | solution.py:574
  10.8 3.7 constant_dynamic-slice_fusion
  26.4 5.7 %load_weights.1 = (bf16[768,3072]{1,0:T(8,128)(2,1)S(1)}, bf16[768,3072]{1,0:T(8,128)(2,1)S(1)}, bf16[3072,768]{1,0:T(8,128)(2,1)S(1)}) custom-call(s32[2]{0:T(128)S(1)} %pad_add_fusion.2.refs_0_, bf16[768,3072]{1,0:T(8,128)(2,1)} %bitcast.225, bf16[768,3072]{1,0:T(8,128)(2,1)} %collective-permute-done.1.refs_2_, bf16[3072,768]{1,0:T(8,128)(2,1)} %bitcast.227, ...), custom_call_target="tpu_custom_call" | custom-call | tf_op jit(solution)/shard_map/load_weights/pallas_call | solution.py:465
  32.1 10.4 %forward_image.8 = (bf16[4,5,208,768]{3,2,1,0:T(8,128)(2,1)}, bf16[4,208,768]{2,1,0:T(8,128)(2,1)S(1)}, bf16[4,208,768]{2,1,0:T(8,128)(2,1)S(1)}, bf16[4,208,768...) custom-call(s32[2]{0:T(128)S(1)} %pad_add_fusion.2.refs_0_, ...), custom_call_target="tpu_custom_call" | custom-call | flops 3107979264 | bytes 12000000 | tf_op jit(solution)/shard_map/forward_image/pallas_call | solution.py:425
  43.8 11.2 %forward_image.9 = (bf16[4,5,208,768]{3,2,1,0:T(8,128)(2,1)}, bf16[4,208,768]{2,1,0:T(8,128)(2,1)S(1)}, bf16[4,208,768]{2,1,0:T(8,128)(2,1)S(1)}, bf16[4,208,768...) custom-call(s32[2]{0:T(128)S(1)} %pad_add_fusion.2.refs_0_, ...), custom_call_target="tpu_custom_call", output_to_operand_aliasing={{0}: (8, {}), {1}: (9, {}), {2}: (10, {}), {3}: (11, {}), {... | custom-call | flops 3107979264 | bytes 12000000 | tf_op jit(solution)/shard_map/forward_image/pallas_call | solution.py:425
  56.3 10.8 %forward_image.10 = (bf16[4,5,208,768]{3,2,1,0:T(8,128)(2,1)}, bf16[4,208,768]{2,1,0:T(8,128)(2,1)S(1)}, bf16[4,208,768]{2,1,0:T(8,128)(2,1)S(1)}, bf16[4,208,76...) custom-call(s32[2]{0:T(128)S(1)} %pad_add_fusion.2.refs_0_, ...), custom_call_target="tpu_custom_call", output_to_operand_aliasing={{0}: (8, {}), {1}: (9, {}), {2}: (10, {}), {3}: (11, {}), {... | custom-call | flops 3107979264 | bytes 12000000 | tf_op jit(solution)/shard_map/forward_image/pallas_call | solution.py:425
  68.4 10.9 %forward_image.11 = (bf16[4,5,208,768]{3,2,1,0:T(8,128)(2,1)}, bf16[4,208,768]{2,1,0:T(8,128)(2,1)S(1)}, bf16[4,208,768]{2,1,0:T(8,128)(2,1)S(1)}, bf16[4,208,76...) custom-call(s32[2]{0:T(128)S(1)} %pad_add_fusion.2.refs_0_, ...), custom_call_target="tpu_custom_call", output_to_operand_aliasing={{0}: (8, {}), {1}: (9, {}), {2}: (10, {}), {3}: (11, {}), {... | custom-call | flops 3107979264 | bytes 12000000 | tf_op jit(solution)/shard_map/forward_image/pallas_call | solution.py:425
  82.4 5.9 %forward_image.13 = (bf16[4,5,208,768]{3,2,1,0:T(8,128)(2,1)}, bf16[4,208,768]{2,1,0:T(8,128)(2,1)S(1)}, bf16[4,208,768]{2,1,0:T(8,128)(2,1)S(1)}, bf16[4,208,76...) custom-call(s32[2]{0:T(128)S(1)} %pad_add_fusion.1.refs_0_, ...), custom_call_target="tpu_custom_call", output_to_operand_aliasing={{0}: (8, {}), {1}: (9, {}), {2}: (10, {}), {3}: (11, {}), {... | custom-call | flops 3107979264 | bytes 12000000 | tf_op jit(solution)/shard_map/forward_image/pallas_call | solution.py:425
  88.3 5.6 %forward_image.14 = (bf16[4,5,208,768]{3,2,1,0:T(8,128)(2,1)}, bf16[4,208,768]{2,1,0:T(8,128)(2,1)S(1)}, bf16[4,208,768]{2,1,0:T(8,128)(2,1)S(1)}, bf16[4,208,76...) custom-call(s32[2]{0:T(128)S(1)} %pad_add_fusion.1.refs_0_, ...), custom_call_target="tpu_custom_call", output_to_operand_aliasing={{0}: (8, {}), {1}: (9, {}), {2}: (10, {}), {3}: (11, {}), {... | custom-call | flops 3107979264 | bytes 12000000 | tf_op jit(solution)/shard_map/forward_image/pallas_call | solution.py:425
  94.0 5.6 %forward_image.15 = (bf16[4,5,208,768]{3,2,1,0:T(8,128)(2,1)}, bf16[4,208,768]{2,1,0:T(8,128)(2,1)S(1)}, bf16[4,208,768]{2,1,0:T(8,128)(2,1)S(1)}, bf16[4,208,76...) custom-call(s32[2]{0:T(128)S(1)} %pad_add_fusion.1.refs_0_, ...), custom_call_target="tpu_custom_call", output_to_operand_aliasing={{0}: (8, {}), {1}: (9, {}), {2}: (10, {}), {3}: (11, {}), {... | custom-call | flops 3107979264 | bytes 12000000 | tf_op jit(solution)/shard_map/forward_image/pallas_call | solution.py:425
  99.6 4.8 %backward_image.8 = (bf16[4,208,3072]{2,1,0:T(8,128)(2,1)S(1)}, bf16[4,208,768]{2,1,0:T(8,128)(2,1)S(1)}, bf16[4,208,768]{2,1,0:T(8,128)(2,1)}, f32[4,8,768]{2,1...) custom-call(s32[2]{0:T(128)S(1)} %pad_add_fusion.1.refs_0_, ...), custom_call_target="tpu_custom_call" | custom-call | flops 3271557120 | bytes 12000000 | tf_op jit(solution)/shard_map/backward_image/pallas_call | solution.py:425
  105.7 4.5 %backward_image.9 = (bf16[4,208,3072]{2,1,0:T(8,128)(2,1)S(1)}, bf16[4,208,768]{2,1,0:T(8,128)(2,1)S(1)}, bf16[4,208,768]{2,1,0:T(8,128)(2,1)}, f32[4,8,768]{2,1...) custom-call(s32[2]{0:T(128)S(1)} %pad_add_fusion.1.refs_0_, ...), custom_call_target="tpu_custom_call", output_to_operand_aliasing={{0}: (12, {}), {1}: (13, {}), {2}: (14, {}), {3}: (15, {}),... | custom-call | flops 3271557120 | bytes 12000000 | tf_op jit(solution)/shard_map/backward_image/pallas_call | solution.py:425
  111.5 4.2 %backward_image.10 = (bf16[4,208,3072]{2,1,0:T(8,128)(2,1)S(1)}, bf16[4,208,768]{2,1,0:T(8,128)(2,1)S(1)}, bf16[4,208,768]{2,1,0:T(8,128)(2,1)}, f32[4,8,768]{2,...) custom-call(s32[2]{0:T(128)S(1)} %pad_add_fusion.1.refs_0_, ...), custom_call_target="tpu_custom_call", output_to_operand_aliasing={{0}: (12, {}), {1}: (13, {}), {2}: (14, {}), {3}: (15, {}),... | custom-call | flops 3271557120 | bytes 12000000 | tf_op jit(solution)/shard_map/backward_image/pallas_call | solution.py:425
  117.0 4.2 %backward_image.11 = (bf16[4,208,3072]{2,1,0:T(8,128)(2,1)S(1)}, bf16[4,208,768]{2,1,0:T(8,128)(2,1)S(1)}, bf16[4,208,768]{2,1,0:T(8,128)(2,1)}, f32[4,8,768]{2,...) custom-call(s32[2]{0:T(128)S(1)} %pad_add_fusion.1.refs_0_, ...), custom_call_target="tpu_custom_call", output_to_operand_aliasing={{0}: (12, {}), {1}: (13, {}), {2}: (14, {}), {3}: (15, {}),... | custom-call | flops 3271557120 | bytes 12000000 | tf_op jit(solution)/shard_map/backward_image/pallas_call | solution.py:425
  122.5 3.5 collective-permute-done.12.refs_1_
  126.0 13.0 %backward_image.12 = (bf16[4,208,3072]{2,1,0:T(8,128)(2,1)S(1)}, bf16[4,208,768]{2,1,0:T(8,128)(2,1)S(1)}, bf16[4,208,768]{2,1,0:T(8,128)(2,1)}, f32[4,8,768]{2,...) custom-call(s32[2]{0:T(128)S(1)} %pad_add_fusion.2.refs_0_, ...), custom_call_target="tpu_custom_call", output_to_operand_aliasing={{0}: (12, {}), {1}: (13, {}), {2}: (14, {}), {3}: (15, {}),... | custom-call | flops 3271557120 | bytes 12000000 | tf_op jit(solution)/shard_map/backward_image/pallas_call | solution.py:425
  139.8 13.0 %backward_image.13 = (bf16[4,208,3072]{2,1,0:T(8,128)(2,1)S(1)}, bf16[4,208,768]{2,1,0:T(8,128)(2,1)S(1)}, bf16[4,208,768]{2,1,0:T(8,128)(2,1)}, f32[4,8,768]{2,...) custom-call(s32[2]{0:T(128)S(1)} %pad_add_fusion.2.refs_0_, ...), custom_call_target="tpu_custom_call", output_to_operand_aliasing={{0}: (12, {}), {1}: (13, {}), {2}: (14, {}), {3}: (15, {}),... | custom-call | flops 3271557120 | bytes 12000000 | tf_op jit(solution)/shard_map/backward_image/pallas_call | solution.py:425
  153.3 13.2 %backward_image.14 = (bf16[4,208,3072]{2,1,0:T(8,128)(2,1)S(1)}, bf16[4,208,768]{2,1,0:T(8,128)(2,1)S(1)}, bf16[4,208,768]{2,1,0:T(8,128)(2,1)}, f32[4,8,768]{2,...) custom-call(s32[2]{0:T(128)S(1)} %pad_add_fusion.2.refs_0_, ...), custom_call_target="tpu_custom_call", output_to_operand_aliasing={{0}: (12, {}), {1}: (13, {}), {2}: (14, {}), {3}: (15, {}),... | custom-call | flops 3271557120 | bytes 12000000 | tf_op jit(solution)/shard_map/backward_image/pallas_call | solution.py:425
  166.9 12.9 %backward_image.15 = (bf16[4,208,3072]{2,1,0:T(8,128)(2,1)S(1)}, bf16[4,208,768]{2,1,0:T(8,128)(2,1)S(1)}, bf16[4,208,768]{2,1,0:T(8,128)(2,1)}, f32[4,8,768]{2,...) custom-call(s32[2]{0:T(128)S(1)} %pad_add_fusion.2.refs_0_, ...), custom_call_target="tpu_custom_call", output_to_operand_aliasing={{0}: (12, {}), {1}: (13, {}), {2}: (14, {}), {3}: (15, {}),... | custom-call | flops 3271557120 | bytes 12000000 | tf_op jit(solution)/shard_map/backward_image/pallas_call | solution.py:425
  179.8 23.9 %weight_parts.1 = (bf16[8,144,768]{2,1,0:T(8,128)(2,1)}, bf16[8,144,768]{2,1,0:T(8,128)(2,1)}, bf16[8,144,768]{2,1,0:T(8,128)(2,1)}, bf16[8,144,768]{2,1,0:T(8,1...) custom-call(s32[2]{0:T(128)S(1)} %pad_add_fusion.3.refs_0_, ...), custom_call_target="tpu_custom_call" | custom-call | flops 1 | bytes 1 | tf_op jit(solution)/shard_map/weight_parts/pallas_call | solution.py:503
  210.3 3.1 table_fold.1
  213.4 4.1 %reshape.271 = f32[12,14,27,14]{3,2,1,0:T(8,128)} reshape(f32[12,14,378]{2,1,0:T(8,128)S(1)} %bitcast.221) | data formatting | bytes 508032 | tf_op jit(solution)/shard_map/reshape | solution.py:528
  228.8 3.3 collective-permute-done.23
  292.1 6.5 %collective-permute-start.46 = (bf16[4,48,768]{2,1,0:T(8,128)(2,1)S(1)}, bf16[4,48,768]{2,1,0:T(8,128)(2,1)S(1)}, u32[]{:S(2)}, u32[]{:S(2)}) collective-permute-start(bf16[4,48,768]{2,1,0:T(8,128)(2,1)S(1)} %pad_maximum_fusion.3), channel_id=1, source_target_pairs={{8,0},{24,16},{9,1},{25,17},{10,2},{26,18},{11,3},{27,19},{12,4},{... | collective-permute-start | bytes 884744 | tf_op jit(solution)/shard_map/ppermute | solution.py:574
  309.3 3.4 collective-permute-start.51
  322.4 3.1 collective-permute-start.57
  350.5 3.2 collective-permute-done.67
  361.2 3.4 collective-permute-done.66.refs_3_
  367.3 3.4 collective-permute-start.70
  382.6 3.3 collective-permute-start.74
  398.1 3.1 collective-permute-start.80
  401.7 3.7 copy.214
  (335 shorter events, 185.5 us)
Async XLA Ops:
  0.6 25.7 %collective-permute-start.1 = (bf16[768,3072]{1,0:T(8,128)(2,1)}, bf16[768,3072]{1,0:T(8,128)(2,1)}, u32[]{:S(2)}, u32[]{:S(2)}) collective-permute-start(bf16[768,3072]{1,0:T(8,128)(2,1)} %bitcast.224), channel_id=1, source_target_pairs={{0,8},{8,0},{16,24},{24,16},{1,9},{9,1},{17,25},{25,17},{2,10},{10... | collective-permute-start | bytes 14155784 | tf_op jit(solution)/shard_map/ppermute | solution.py:574
  0.8 25.6 %collective-permute-start.2 = (bf16[3072,768]{1,0:T(8,128)(2,1)}, bf16[3072,768]{1,0:T(8,128)(2,1)}, u32[]{:S(2)}, u32[]{:S(2)}) collective-permute-start(bf16[3072,768]{1,0:T(8,128)(2,1)} %bitcast.226), channel_id=1, source_target_pairs={{8,0},{24,16},{9,1},{25,17},{10,2},{26,18},{11,3},{27,19},{12,4},{... | collective-permute-start | bytes 14155784 | tf_op jit(solution)/shard_map/ppermute | solution.py:574
  6.1 11.7 %collective-permute-start.3 = (f32[12,732]{1,0:T(8,128)S(1)}, f32[12,732]{1,0:T(8,128)S(1)}, u32[]{:S(2)}, u32[]{:S(2)}) collective-permute-start(f32[12,732]{1,0:T(8,128)S(1)} %bitcast.234), channel_id=1, source_target_pairs={{0,8},{16,24},{1,9},{17,25},{2,10},{18,26},{3,11},{19,27},{4,12},{... | collective-permute-start | bytes 105416 | tf_op jit(solution)/shard_map/ppermute | solution.py:574
  42.5 38.1 %collective-permute-start.7 = (bf16[208,768]{1,0:T(8,128)(2,1)S(1)}, bf16[208,768]{1,0:T(8,128)(2,1)S(1)}, u32[]{:S(2)}, u32[]{:S(2)}) collective-permute-start(bf16[208,768]{1,0:T(8,128)(2,1)S(1)} %get-tuple-element.301), channel_id=1, source_target_pairs={{0,16},{8,24},{1,17},{9,25},{2,18},{10,26},{3,19},{11,27},{4,20},{... | collective-permute-start | bytes 958472 | tf_op jit(solution)/shard_map/ppermute | solution.py:574
  55.0 27.4 %collective-permute-start.6 = (bf16[208,768]{1,0:T(8,128)(2,1)S(1)}, bf16[208,768]{1,0:T(8,128)(2,1)S(1)}, u32[]{:S(2)}, u32[]{:S(2)}) collective-permute-start(bf16[208,768]{1,0:T(8,128)(2,1)S(1)} %get-tuple-element.300), channel_id=1, source_target_pairs={{0,16},{8,24},{1,17},{9,25},{2,18},{10,26},{3,19},{11,27},{4,20},{... | collective-permute-start | bytes 958472 | tf_op jit(solution)/shard_map/ppermute | solution.py:574
  67.1 21.2 %collective-permute-start.5 = (bf16[208,768]{1,0:T(8,128)(2,1)S(1)}, bf16[208,768]{1,0:T(8,128)(2,1)S(1)}, u32[]{:S(2)}, u32[]{:S(2)}) collective-permute-start(bf16[208,768]{1,0:T(8,128)(2,1)S(1)} %get-tuple-element.299), channel_id=1, source_target_pairs={{0,16},{8,24},{1,17},{9,25},{2,18},{10,26},{3,19},{11,27},{4,20},{... | collective-permute-start | bytes 958472 | tf_op jit(solution)/shard_map/ppermute | solution.py:574
  79.3 14.6 %collective-permute-start.4 = (bf16[208,768]{1,0:T(8,128)(2,1)S(1)}, bf16[208,768]{1,0:T(8,128)(2,1)S(1)}, u32[]{:S(2)}, u32[]{:S(2)}) collective-permute-start(bf16[208,768]{1,0:T(8,128)(2,1)S(1)} %get-tuple-element.298), channel_id=1, source_target_pairs={{0,16},{8,24},{1,17},{9,25},{2,18},{10,26},{3,19},{11,27},{4,20},{... | collective-permute-start | bytes 958472 | tf_op jit(solution)/shard_map/ppermute | solution.py:574
  104.4 21.6 %collective-permute-start.12 = (bf16[208,768]{1,0:T(8,128)(2,1)S(1)}, bf16[208,768]{1,0:T(8,128)(2,1)S(1)}, u32[]{:S(2)}, u32[]{:S(2)}) collective-permute-start(bf16[208,768]{1,0:T(8,128)(2,1)S(1)} %get-tuple-element.379), channel_id=1, source_target_pairs={{16,0},{24,8},{17,1},{25,9},{18,2},{26,10},{19,3},{27,11},{20,4},{... | collective-permute-start | bytes 958472 | tf_op jit(solution)/shard_map/ppermute | solution.py:574
  110.2 29.6 %collective-permute-start.11 = (bf16[208,768]{1,0:T(8,128)(2,1)S(1)}, bf16[208,768]{1,0:T(8,128)(2,1)S(1)}, u32[]{:S(2)}, u32[]{:S(2)}) collective-permute-start(bf16[208,768]{1,0:T(8,128)(2,1)S(1)} %get-tuple-element.378), channel_id=1, source_target_pairs={{16,0},{24,8},{17,1},{25,9},{18,2},{26,10},{19,3},{27,11},{20,4},{... | collective-permute-start | bytes 958472 | tf_op jit(solution)/shard_map/ppermute | solution.py:574
  115.7 37.6 %collective-permute-start.10 = (bf16[208,768]{1,0:T(8,128)(2,1)S(1)}, bf16[208,768]{1,0:T(8,128)(2,1)S(1)}, u32[]{:S(2)}, u32[]{:S(2)}) collective-permute-start(bf16[208,768]{1,0:T(8,128)(2,1)S(1)} %get-tuple-element.377), channel_id=1, source_target_pairs={{16,0},{24,8},{17,1},{25,9},{18,2},{26,10},{19,3},{27,11},{20,4},{... | collective-permute-start | bytes 958472 | tf_op jit(solution)/shard_map/ppermute | solution.py:574
  121.2 45.7 %collective-permute-start.9 = (bf16[208,768]{1,0:T(8,128)(2,1)S(1)}, bf16[208,768]{1,0:T(8,128)(2,1)S(1)}, u32[]{:S(2)}, u32[]{:S(2)}) collective-permute-start(bf16[208,768]{1,0:T(8,128)(2,1)S(1)} %get-tuple-element.376), channel_id=1, source_target_pairs={{16,0},{24,8},{17,1},{25,9},{18,2},{26,10},{19,3},{27,11},{20,4},{... | collective-permute-start | bytes 958472 | tf_op jit(solution)/shard_map/ppermute | solution.py:574
  203.7 16.4 %collective-permute-start.14 = (bf16[8,144,768]{2,1,0:T(8,128)(2,1)}, bf16[8,144,768]{2,1,0:T(8,128)(2,1)S(1)}, u32[]{:S(2)}, u32[]{:S(2)}) collective-permute-start(bf16[8,144,768]{2,1,0:T(8,128)(2,1)} %get-tuple-element.435), channel_id=1, source_target_pairs={{0,8},{8,0},{16,24},{24,16},{1,9},{9,1},{17,25},{25,17},{2,10},{10... | collective-permute-start | bytes 5308424 | tf_op jit(solution)/shard_map/ppermute | solution.py:574
  207.0 14.7 %collective-permute-start.22 = (bf16[8,144,768]{2,1,0:T(8,128)(2,1)}, bf16[8,144,768]{2,1,0:T(8,128)(2,1)}, u32[]{:S(2)}, u32[]{:S(2)}) collective-permute-start(bf16[8,144,768]{2,1,0:T(8,128)(2,1)} %get-tuple-element.437), channel_id=1, source_target_pairs={{0,8},{8,0},{16,24},{24,16},{1,9},{9,1},{17,25},{25,17},{2,10},{10... | collective-permute-start | bytes 5308424 | tf_op jit(solution)/shard_map/ppermute | solution.py:574
  207.1 16.9 %collective-permute-start.30 = (bf16[8,144,768]{2,1,0:T(8,128)(2,1)}, bf16[8,144,768]{2,1,0:T(8,128)(2,1)}, u32[]{:S(2)}, u32[]{:S(2)}) collective-permute-start(bf16[8,144,768]{2,1,0:T(8,128)(2,1)} %get-tuple-element.439), channel_id=1, source_target_pairs={{0,8},{8,0},{16,24},{24,16},{1,9},{9,1},{17,25},{25,17},{2,10},{10... | collective-permute-start | bytes 5308424 | tf_op jit(solution)/shard_map/ppermute | solution.py:574
  207.6 17.7 %collective-permute-start.38 = (bf16[8,144,768]{2,1,0:T(8,128)(2,1)}, bf16[8,144,768]{2,1,0:T(8,128)(2,1)}, u32[]{:S(2)}, u32[]{:S(2)}) collective-permute-start(bf16[8,144,768]{2,1,0:T(8,128)(2,1)} %get-tuple-element.441), channel_id=1, source_target_pairs={{0,8},{8,0},{16,24},{24,16},{1,9},{9,1},{17,25},{25,17},{2,10},{10... | collective-permute-start | bytes 5308424 | tf_op jit(solution)/shard_map/ppermute | solution.py:574
  209.8 95.8 %collective-permute-start.52 = (f32[8,768]{1,0:T(8,128)S(1)}, f32[8,768]{1,0:T(8,128)S(1)}, u32[]{:S(2)}, u32[]{:S(2)}) collective-permute-start(f32[8,768]{1,0:T(8,128)S(1)} %broadcast_select_fusion.9), channel_id=1, source_target_pairs={{0,8},{8,0},{16,24},{24,16},{1,9},{9,1},{17,25},{25,17},{2,10},{10... | collective-permute-start | bytes 73736 | tf_op jit(solution)/shard_map/ppermute | solution.py:574
  312.9 13.9 %collective-permute-start.58 = (f32[120,128]{1,0:T(8,128)S(1)}, f32[120,128]{1,0:T(8,128)S(1)}, u32[]{:S(2)}, u32[]{:S(2)}) collective-permute-start(f32[120,128]{1,0:T(8,128)S(1)} %maximum_bitcast_fusion), channel_id=1, source_target_pairs={{0,1},{1,0},{2,3},{3,2},{4,5},{5,4},{6,7},{7,6},{8,9},{9,8},{10,11... | collective-permute-start | bytes 184328 | tf_op jit(solution)/shard_map/ppermute | solution.py:649
  318.7 12.0 %collective-permute-start.54 = (bf16[2,96,768]{2,1,0:T(8,128)(2,1)S(1)}, bf16[2,96,768]{2,1,0:T(8,128)(2,1)S(1)}, u32[]{:S(2)}, u32[]{:S(2)}) collective-permute-start(bf16[2,96,768]{2,1,0:T(8,128)(2,1)S(1)} %collective-permute-done.47.refs_2_), channel_id=1, source_target_pairs={{0,1},{2,0},{4,2},{6,4},{7,6},{5,7},{3,5},{1,3},{8,9},{10,8},{12,1... | collective-permute-start | bytes 884744 | tf_op jit(solution)/shard_map/ppermute | solution.py:644
  319.0 11.8 %collective-permute-start.55 = (bf16[2,96,768]{2,1,0:T(8,128)(2,1)S(1)}, bf16[2,96,768]{2,1,0:T(8,128)(2,1)S(1)}, u32[]{:S(2)}, u32[]{:S(2)}) collective-permute-start(bf16[2,96,768]{2,1,0:T(8,128)(2,1)S(1)} %collective-permute-done.48.refs_1_), channel_id=1, source_target_pairs={{0,2},{2,4},{4,6},{6,7},{7,5},{5,3},{3,1},{1,0},{8,10},{10,12},{12... | collective-permute-start | bytes 884744 | tf_op jit(solution)/shard_map/ppermute | solution.py:644
  326.7 43.9 %collective-permute-start.8 = (bf16[4,208,768]{2,1,0:T(8,128)(2,1)}, bf16[4,208,768]{2,1,0:T(8,128)(2,1)}, u32[]{:S(2)}, u32[]{:S(2)}) collective-permute-start(bf16[4,208,768]{2,1,0:T(8,128)(2,1)} %broadcast_select_fusion.6), channel_id=1, source_target_pairs={{0,8},{8,0},{16,24},{24,16},{1,9},{9,1},{17,25},{25,17},{2,10},{10... | collective-permute-start | bytes 3833864 | tf_op jit(solution)/shard_map/ppermute | solution.py:574
  331.8 11.6 %collective-permute-start.60 = (bf16[2,96,768]{2,1,0:T(8,128)(2,1)S(1)}, bf16[2,96,768]{2,1,0:T(8,128)(2,1)S(1)}, u32[]{:S(2)}, u32[]{:S(2)}) collective-permute-start(bf16[2,96,768]{2,1,0:T(8,128)(2,1)S(1)} %collective-permute-done.55.refs_1_), channel_id=1, source_target_pairs={{0,2},{2,4},{4,6},{6,7},{7,5},{5,3},{3,1},{1,0},{8,10},{10,12},{12... | collective-permute-start | bytes 884744 | tf_op jit(solution)/shard_map/ppermute | solution.py:644
  332.3 11.1 %collective-permute-start.61 = (bf16[2,96,768]{2,1,0:T(8,128)(2,1)S(1)}, bf16[2,96,768]{2,1,0:T(8,128)(2,1)S(1)}, u32[]{:S(2)}, u32[]{:S(2)}) collective-permute-start(bf16[2,96,768]{2,1,0:T(8,128)(2,1)S(1)} %collective-permute-done.56.refs_4_), channel_id=1, source_target_pairs={{8,9},{10,8},{12,10},{14,12},{15,14},{13,15},{11,13},{9,11},{24,25... | collective-permute-start | bytes 884744 | tf_op jit(solution)/shard_map/ppermute | solution.py:645
  338.9 47.0 %collective-permute-start.13 = (bf16[4,208,768]{2,1,0:T(8,128)(2,1)}, bf16[4,208,768]{2,1,0:T(8,128)(2,1)}, u32[]{:S(2)}, u32[]{:S(2)}) collective-permute-start(bf16[4,208,768]{2,1,0:T(8,128)(2,1)} %broadcast_select_fusion.2), channel_id=1, source_target_pairs={{0,8},{8,0},{16,24},{24,16},{1,9},{9,1},{17,25},{25,17},{2,10},{10... | collective-permute-start | bytes 3833864 | tf_op jit(solution)/shard_map/ppermute | solution.py:574
  343.6 12.5 %collective-permute-start.63 = (bf16[2,96,768]{2,1,0:T(8,128)(2,1)S(1)}, bf16[2,96,768]{2,1,0:T(8,128)(2,1)S(1)}, u32[]{:S(2)}, u32[]{:S(2)}) collective-permute-start(bf16[2,96,768]{2,1,0:T(8,128)(2,1)S(1)} %collective-permute-done.59.refs_2_), channel_id=1, source_target_pairs={{0,1},{2,0},{4,2},{6,4},{7,6},{5,7},{3,5},{1,3},{8,9},{10,8},{12,1... | collective-permute-start | bytes 884744 | tf_op jit(solution)/shard_map/ppermute | solution.py:644
  349.0 12.1 %collective-permute-start.64 = (bf16[2,96,768]{2,1,0:T(8,128)(2,1)S(1)}, bf16[2,96,768]{2,1,0:T(8,128)(2,1)S(1)}, u32[]{:S(2)}, u32[]{:S(2)}) collective-permute-start(bf16[2,96,768]{2,1,0:T(8,128)(2,1)S(1)} %collective-permute-done.60.refs_1_), channel_id=1, source_target_pairs={{0,2},{2,4},{4,6},{6,7},{7,5},{5,3},{3,1},{1,0},{8,10},{10,12},{12... | collective-permute-start | bytes 884744 | tf_op jit(solution)/shard_map/ppermute | solution.py:644
  364.6 13.6 %collective-permute-start.68 = (bf16[2,96,768]{2,1,0:T(8,128)(2,1)S(1)}, bf16[2,96,768]{2,1,0:T(8,128)(2,1)S(1)}, u32[]{:S(2)}, u32[]{:S(2)}) collective-permute-start(bf16[2,96,768]{2,1,0:T(8,128)(2,1)S(1)} %collective-permute-done.63.refs_2_), channel_id=1, source_target_pairs={{0,1},{2,0},{4,2},{6,4},{7,6},{5,7},{3,5},{1,3},{8,9},{10,8},{12,1... | collective-permute-start | bytes 884744 | tf_op jit(solution)/shard_map/ppermute | solution.py:644
  367.3 11.7 %collective-permute-start.69 = (bf16[2,96,768]{2,1,0:T(8,128)(2,1)S(1)}, bf16[2,96,768]{2,1,0:T(8,128)(2,1)S(1)}, u32[]{:S(2)}, u32[]{:S(2)}) collective-permute-start(bf16[2,96,768]{2,1,0:T(8,128)(2,1)S(1)} %collective-permute-done.64.refs_1_), channel_id=1, source_target_pairs={{0,2},{2,4},{4,6},{6,7},{7,5},{5,3},{3,1},{1,0},{8,10},{10,12},{12... | collective-permute-start | bytes 884744 | tf_op jit(solution)/shard_map/ppermute | solution.py:644
  367.3 11.7 %collective-permute-start.70 = (bf16[2,96,768]{2,1,0:T(8,128)(2,1)S(1)}, bf16[2,96,768]{2,1,0:T(8,128)(2,1)S(1)}, u32[]{:S(2)}, u32[]{:S(2)}) collective-permute-start(bf16[2,96,768]{2,1,0:T(8,128)(2,1)S(1)} %collective-permute-done.65.refs_4_), channel_id=1, source_target_pairs={{8,9},{10,8},{12,10},{14,12},{15,14},{13,15},{11,13},{9,11},{24,25... | collective-permute-start | bytes 884744 | tf_op jit(solution)/shard_map/ppermute | solution.py:645
  378.2 13.3 %collective-permute-start.76 = (f32[120,128]{1,0:T(8,128)S(1)}, f32[120,128]{1,0:T(8,128)S(1)}, u32[]{:S(2)}, u32[]{:S(2)}) collective-permute-start(f32[120,128]{1,0:T(8,128)S(1)} %add.564), channel_id=1, source_target_pairs={{0,4},{1,5},{2,6},{3,7},{4,0},{5,1},{6,2},{7,3},{8,12},{9,13},{10,... | collective-permute-start | bytes 184328 | tf_op jit(solution)/shard_map/ppermute | solution.py:649
  394.4 13.0 %collective-permute-start.77 = (bf16[2,96,768]{2,1,0:T(8,128)(2,1)S(1)}, bf16[2,96,768]{2,1,0:T(8,128)(2,1)S(1)}, u32[]{:S(2)}, u32[]{:S(2)}) collective-permute-start(bf16[2,96,768]{2,1,0:T(8,128)(2,1)S(1)} %collective-permute-done.72.refs_2_), channel_id=1, source_target_pairs={{0,1},{2,0},{4,2},{6,4},{7,6},{5,7},{3,5},{1,3},{8,9},{10,8},{12,1... | collective-permute-start | bytes 884744 | tf_op jit(solution)/shard_map/ppermute | solution.py:644
  394.7 12.7 %collective-permute-start.78 = (bf16[2,96,768]{2,1,0:T(8,128)(2,1)S(1)}, bf16[2,96,768]{2,1,0:T(8,128)(2,1)S(1)}, u32[]{:S(2)}, u32[]{:S(2)}) collective-permute-start(bf16[2,96,768]{2,1,0:T(8,128)(2,1)S(1)} %collective-permute-done.73.refs_1_), channel_id=1, source_target_pairs={{0,2},{2,4},{4,6},{6,7},{7,5},{5,3},{3,1},{1,0},{8,10},{10,12},{12... | collective-permute-start | bytes 884744 | tf_op jit(solution)/shard_map/ppermute | solution.py:644
  395.9 11.6 %collective-permute-start.79 = (bf16[2,96,768]{2,1,0:T(8,128)(2,1)S(1)}, bf16[2,96,768]{2,1,0:T(8,128)(2,1)S(1)}, u32[]{:S(2)}, u32[]{:S(2)}) collective-permute-start(bf16[2,96,768]{2,1,0:T(8,128)(2,1)S(1)} %collective-permute-done.74.refs_4_), channel_id=1, source_target_pairs={{8,9},{10,8},{12,10},{14,12},{15,14},{13,15},{11,13},{9,11},{24,25... | collective-permute-start | bytes 884744 | tf_op jit(solution)/shard_map/ppermute | solution.py:645
  (69 other events, 640.2 us)
where the time goes:
time: 419 us; the launch traced here: 411 us
  Pallas kernels  183 us (44%)
  starting transfers between devices  107 us (26%)
  waiting for transfers between devices  45.1 us (11%)
  other arithmetic  36.8 us (9%)
  local copies, waits for them, and re-layouts  29.2 us (7%)
  between operations  10.6 us (3%)
    pallas_call x16, Pallas kernels, run(): pl.pallas_call(kernel, out_shape=tuple(shapes) + tuple(extra), in_specs=l...  132 us
    ppermute x14, starting transfers between devices, weight_sums(): lax.ppermute(b[w], ('section', axis), upper[w])  37.1 us
    ppermute x22, starting transfers between devices, swap(): return lax.ppermute(block, 'section', pairs)  32.5 us
    convert_element_type x32, other arithmetic, weight_sums(): held[s] = total.astype(BF)  25.4 us
    pallas_call x1, Pallas kernels, parts(): pl.pallas_call(lambda *refs: weight_parts(ups, refs[:9], refs[9:13], refs...  23.9 us
    ppermute x28, waiting for transfers between devices, weight_sums(): lax.ppermute(held[s], axis, route[1 if s < 2 else -1]).astype(F32)  23.2 us
    ppermute x28, starting transfers between devices, weight_sums(): lax.ppermute(held[s], axis, route[1 if s < 2 else -1]).astype(F32)  23 us
    pallas_call x8, Pallas kernels, place(): pl.pallas_call(lambda *refs: place_sums(refs[:5], refs[5 + given:7 + give...  16.3 us
  transfers between devices with their start and end apart: 81, of which 30 were waited for; matrix products, arithmetic and copies ran while one was open for 16% of the time, Pallas kernels for 29%

commit v1 on v0

--- a/solution.py
+++ b/solution.py
@@ -46,13 +46,8 @@
 
 
 def gelu_parts(h):
-    z = jnp.abs(h) * 0.7071067811865476
-    t = 1.0 / (1.0 + 0.3275911 * z)
-    gauss = jnp.exp(-0.5 * h * h)
-    poly = t * (0.127414796 + t * (-0.142248368 + t * (0.7107068705 + t * (-0.7265760135 + t * 0.5307027145))))
-    tail = poly * gauss
-    phi = jnp.where(h >= 0.0, 1.0 - tail, tail)
-    return h * phi, phi + h * (gauss * 0.3989422804014327)
+    phi = 0.5 + 0.5 * lax.erf(h * 0.7071067811865476)
+    return h * phi, phi + h * (jnp.exp(-0.5 * h * h) * 0.3989422804014327)
 
 
 class Copies:
@@ -66,21 +61,27 @@
         return copy
 
     def choose(self, first, a, b, dst):
+        return self.either(first, (a, dst), (b, dst))
+
+    def either(self, first, one, two):
         sem = self.sems.at[self.used]
         self.used += 1
 
         @pl.when(first)
         def _():
-            pltpu.make_async_copy(a, dst, sem).start()
+            pltpu.make_async_copy(*one, sem).start()
 
         @pl.when(jnp.logical_not(first))
         def _():
-            pltpu.make_async_copy(b, dst, sem).start()
-
-        return pltpu.make_async_copy(a, dst, sem)
+            pltpu.make_async_copy(*two, sem).start()
+
+        return pltpu.make_async_copy(*one, sem)
 
     def store(self, src, dst):
         self.out.append(self.start(src, dst))
+
+    def store_choose(self, first, src, a, b):
+        self.out.append(self.either(first, (src, a), (src, b)))
 
     def finish(self):
         for copy in self.out:
@@ -99,19 +100,36 @@
 
 
 def forward_image(i, refs_in, refs_state, refs_extra, scratch):
-    flags, x_ref, vec_ref, vecf_ref, wa_ref, w1_ref, w2_ref, bias_ref = refs_in
+    flags, x_ref, vec_ref, vecf_ref, bias_ref = refs_in[:5]
+    loading = len(refs_in) > 8
+    wa_ref, w1_ref, w2_ref = refs_extra[1:] if loading else refs_in[5:]
     x_ref = image_of(x_ref, i)
-    sa, a1, ctx, y1, pb, g_all, a2, gp, b2, y2 = refs_state
-    (send,) = refs_extra
+    sa, a1, ctx, y1, pb, g_all, a2, gp, b2, keep, give = refs_state
+    core_first = flags[1] == 0
+    send = refs_extra[0]
     x_v, qkv_v, pb_v, b_v, y_v, gp_v, bf_v, yf_v, sems = scratch
     rows, width = x_v.shape
     heads, keys = pb_v.shape[0], pb_v.shape[2]
     hidden = gp_v.shape[1]
     a_v, c_v, g_v, af_v = a1.at[i], ctx.at[i], g_all.at[i], a2.at[i]
+    cp = Copies(sems)
+    ready = []
+    if loading:
+        own_ref, other_ref, own_d, other_d = refs_in[5:]
+        first = flags[1] == 0
+        ready = [
+            cp.choose(first, own_ref, other_ref, wa_ref),
+            cp.choose(first, other_ref, own_ref, w1_ref),
+            cp.choose(first, other_d, own_d, w2_ref),
+        ]
+
+        @pl.when(flags[0] == 0)
+        def _():
+            for copy in ready:
+                copy.wait()
 
     @pl.when(flags[0] == 1)
     def _():
-        cp = Copies(sems)
         x_v[...] = x_ref[...]
         cp.store(x_v, sa.at[i, 0])
         xhat, rstd = norm_stats(x_v[...].astype(F32))
@@ -119,6 +137,8 @@
         qkv_v[rows:, :] = jnp.zeros((keys - rows, 3 * width), BF)
         a = a_v[...]
         block = 256
+        if loading:
+            ready[0].wait()
         for j in range(3 * width // block):
             cols = slice(j * block, (j + 1) * block)
             part = dot(a, wa_ref[:, cols])
@@ -136,14 +156,14 @@
             q = qkv_v[0:rows, j * 128 : (j + 1) * 128]
             k = qkv_v[:, width + j * 128 : width + (j + 1) * 128]
             u = qkv_v[:, 2 * width + j * 128 : 2 * width + (j + 1) * 128]
-            total = None
+            soft = []
             for t in range(2):
                 s = dot_nt(q * scaled[t], k) + bias_ref[2 * j + t]
                 e = jnp.exp(s - jnp.max(s, -1, keepdims=True))
                 p = (e * (1.0 / jnp.sum(e, -1, keepdims=True))).astype(BF)
                 pb_v[2 * j + t] = p
-                part = dot(p, u * plain[t])
-                total = part if total is None else total + part
+                soft.append(p)
+            total = dot(jnp.concatenate(soft, 1), jnp.concatenate([u * plain[0], u * plain[1]], 0))
             c_v[:, j * 128 : (j + 1) * 128] = total.astype(BF)
         cp.store(pb_v, pb.at[i])
         b = dot(c_v[...], wa_ref[:, 3 * width :]) + vec_ref[3:4, :]
@@ -151,10 +171,13 @@
         cp.store(b_v, sa.at[i, 4])
         y_v[...] = (x_v[...].astype(F32) + vec_ref[2:3, :] * b).astype(BF)
         cp.store(y_v, y1.at[i])
+        cp.store_choose(core_first, y_v, keep.at[i], give.at[i])
 
         xhat, rstd = norm_stats(y_v[...].astype(F32))
         af_v[...] = (xhat * vecf_ref[0:1, :] + vecf_ref[1:2, :]).astype(BF)
         a = af_v[...]
+        if loading:
+            ready[1].wait()
         for j in range(hidden // block):
             row, at = divmod(j * block, width)
             cols = slice(j * block, (j + 1) * block)
@@ -163,19 +186,22 @@
             g_v[:, cols] = value.astype(BF)
             gp_v[:, cols] = slope.astype(BF)
         cp.store(gp_v, gp.at[i])
+        if loading:
+            ready[2].wait()
         b = dot(g_v[...], w2_ref[...]) + vecf_ref[3:4, :]
         yf_v[...] = (y_v[...].astype(F32) + vecf_ref[2:3, :] * b).astype(BF)
         send[...] = yf_v[...]
-        cp.store(yf_v, y2.at[i])
+        cp.store_choose(core_first, yf_v, give.at[i], keep.at[i])
         bf_v[...] = b.astype(BF)
         cp.store(bf_v, b2.at[i])
         cp.finish()
 
 
 def backward_image(i, refs_in, refs_state, refs_extra, scratch):
-    flags, g_ref, vec_ref, vecf_ref, wa_ref, w1_ref, w2_ref, sa, pb, y1, gp, b2 = refs_in
+    flags, g_ref, vec_ref, vecf_ref, wa_ref, w1_ref, w2_ref, hide_ref, sa, pb, y1, gp, b2 = refs_in
     g_ref = image_of(g_ref, i)
-    dh_all, ef, dx1, vgf, ea, dq, dl, dx0, vga = refs_state
+    dh_all, ef, keep, vgf, ea, dq, dl, give, vga = refs_state
+    core_first = flags[1] == 0
     (send,) = refs_extra
     (gin_v, gp_v, bf_v, xf_v, qkv_v, pb_v, b_v, x_v, dx_v, vgf_v, dc_v, dl_v, dx0_v, vg_v, sems) = scratch
     e_v, dh_v, ea_v, dq_v = ef.at[i], dh_all.at[i], ea.at[i], dq.at[i]
@@ -194,7 +220,7 @@
         in_b = cp.start(sa.at[i, 4], b_v)
         in_x = cp.start(sa.at[i, 0], x_v)
         qkv_v[rows:, :] = jnp.zeros((keys - rows, 3 * width), BF)
-        vg_v[6:8, :] = jnp.zeros((2, width), F32)
+        vg_v[7:8, :] = jnp.zeros((1, width), F32)
         gin_v[...] = g_ref[...]
         scaled = gin_v[...].astype(F32) * vecf_ref[2:3, :]
         e_v[...] = scaled.astype(BF)
@@ -217,7 +243,7 @@
         vgf_v[1:2, :] = rows_sum(da)
         cp.store(vgf_v, vgf.at[i])
         dx_v[...] = norm_back(gin_v[...].astype(F32), da, xhat, rstd, vecf_ref[0:1, :]).astype(BF)
-        cp.store(dx_v, dx1.at[i])
+        cp.store_choose(core_first, dx_v, give.at[i], keep.at[i])
 
         scaled = dx_v[...].astype(F32) * vec_ref[2:3, :]
         ea_v[...] = scaled.astype(BF)
@@ -234,22 +260,20 @@
             k = qkv_v[:, width + j * 128 : width + (j + 1) * 128]
             u = qkv_v[:, 2 * width + j * 128 : 2 * width + (j + 1) * 128]
             dc = dc_v[:, cols]
-            dq_t, dk_t, du_t = None, None, None
-            for t in range(2):
-                dc_t = dc * plain[t]
-                p = pb_v[2 * j + t]
-                dp = dot_nt(dc_t, u)
-                pf = p.astype(F32)
-                wp = pf * dp
-                ds = wp - pf * jnp.sum(wp, -1, keepdims=True)
-                dlog = (ds * factor).astype(BF)
-                dl_v[2 * j + t] = dlog
-                du = dot_tn(p, dc_t)
-                dqp = dot(dlog, k * plain[t])
-                dkp = dot_tn(dlog, q * plain[t])
-                dq_t = dqp if dq_t is None else dq_t + dqp
-                dk_t = dkp if dk_t is None else dk_t + dkp
-                du_t = du if du_t is None else du_t + du
+            dcs = jnp.concatenate([dc * plain[0], dc * plain[1]], 0)
+            probs = pb_v[2 * j : 2 * j + 2].reshape(2 * rows, keys)
+            dp = dot_nt(dcs, u)
+            pf = probs.astype(F32)
+            wp = pf * dp
+            ds = wp - pf * jnp.sum(wp, -1, keepdims=True)
+            dlog = (ds * factor).astype(BF)
+            dl_v[2 * j : 2 * j + 2] = dlog.reshape(2, rows, keys)
+            du_t = dot_tn(probs, dcs)
+            dq_t = dot(
+                jnp.concatenate([dlog[:rows], dlog[rows:]], 1),
+                jnp.concatenate([k * plain[0], k * plain[1]], 0),
+            )
+            dk_t = dot_tn(dlog, jnp.concatenate([q * plain[0], q * plain[1]], 0))
             dq_v[:, j * 128 : (j + 1) * 128] = dq_t.astype(BF)
             dq_v[:, width + j * 128 : width + (j + 1) * 128] = dk_t[0:rows].astype(BF)
             dq_v[:, 2 * width + j * 128 : 2 * width + (j + 1) * 128] = du_t[0:rows].astype(BF)
@@ -261,26 +285,16 @@
         vg_v[2:3, :] = rows_sum(dx_v[...].astype(F32) * b_v[...].astype(F32))
         da = dot_nt(dq_v[...], wa_ref[:, 0 : 3 * width])
         xhat, rstd = norm_stats(x_v[...].astype(F32))
-        dx0_v[...] = norm_back(dx_v[...].astype(F32), da, xhat, rstd, vec_ref[0:1, :]).astype(BF)
-        send[...] = dx0_v[...]
-        cp.store(dx0_v, dx0.at[i])
+        dx = norm_back(dx_v[...].astype(F32), da, xhat, rstd, vec_ref[0:1, :])
+        send[...] = dx.astype(BF)
+        hidden_rows = hide_ref[i] > 0.0
+        dx0_v[...] = jnp.where(hidden_rows, 0.0, dx).astype(BF)
+        vg_v[6:7, :] = rows_sum(jnp.where(hidden_rows, dx, 0.0))
+        cp.store_choose(core_first, dx0_v, keep.at[i], give.at[i])
         vg_v[0:1, :] = rows_sum(da * xhat)
         vg_v[1:2, :] = rows_sum(da)
         cp.store(vg_v, vga.at[i])
         cp.finish()
-
-
-def load_weights(refs_in, refs_out, scratch):
-    flags, own_ref, other_ref, own_d, other_d = refs_in
-    wa_ref, w1_ref, w2_ref = refs_out
-    first = flags[1] == 0
-    cp = Copies(scratch[0])
-    for copy in (
-        cp.choose(first, own_ref, other_ref, wa_ref),
-        cp.choose(first, other_ref, own_ref, w1_ref),
-        cp.choose(first, other_d, own_d, w2_ref),
-    ):
-        copy.wait()
 
 
 def weight_parts(ups, refs_in, sents, owns, scratch):
@@ -292,20 +306,17 @@
     cp = Copies(sems)
     core, at = flags[0], flags[1]
     low = core == 0
-    cuts = 2
+    cuts = 1
     block, group = width // cuts, chunks // cuts
     rows = a2.shape[0] * a2.shape[1]
 
     def product(left, right, first_col, second_col, put):
         rhs = right[:, :, second_col : second_col + width].reshape(rows, width)
 
-        def one(k, none):
-            start = pl.multiple_of(first_col + k * block, 128)
-            lhs = left[:, :, pl.ds(start, block)].reshape(rows, block)
+        for k in range(cuts):
+            start = first_col + k * block
+            lhs = left[:, :, start : start + block].reshape(rows, block)
             put(pl.ds(k * group, group), dot_tn(lhs, rhs).astype(BF).reshape(group, tall, width))
-            return none
-
-        lax.fori_loop(0, cuts, one, 0)
 
     def share(turn, s, which, target):
         def put(group, value):
@@ -344,32 +355,67 @@
     cp.finish()
 
 
-def table_fold(grid, dl, by_col, edge, dl_v, sems):
+def join_images(refs_in, out, scratch):
+    flags, keep_ref, got_ref = refs_in
+    all_v, sems = scratch
+    half = keep_ref.shape[0]
+    cp = Copies(sems)
+    low = flags[0] == 0
+    copies = [
+        cp.choose(low, keep_ref, got_ref, all_v.at[0:half]),
+        cp.choose(low, got_ref, keep_ref, all_v.at[half : 2 * half]),
+    ]
+    for copy in copies:
+        copy.wait()
+    length, size = out.shape[0], 16
+    for at in range(0, length, size):
+        n = min(size, length - at)
+        block = jnp.swapaxes(all_v[:, at : at + size, :].astype(F32), 0, 1)
+        out[at : at + n] = block[:n].astype(out.dtype)
+
+
+def table_fold(grid, dl, out, dl_v, sems):
     images, heads, rows, keys = dl.shape
-    patches = grid * grid
-    wide = by_col.shape[2]
+    patches, side = grid * grid, 2 * grid - 1
+    wide = -(-(side * grid) // 128) * 128 + 128
     copies = []
     for h in range(heads):
         copy = pltpu.make_async_copy(dl.at[:, h], dl_v.at[h], sems.at[h])
         copy.start()
         copies.append(copy)
     lane = lax.broadcasted_iota(jnp.int32, (1, keys), 1)
-    inner = lane > 0
+    narrow = lax.broadcasted_iota(jnp.int32, (1, 256), 1)
+    last = lax.broadcasted_iota(jnp.int32, (1, out.shape[1]), 1)
     for h in range(heads):
         copies[h].wait()
         total = dl_v[h, 0].astype(F32)
         for i in range(1, images):
             total = total + dl_v[h, i].astype(F32)
-        edge[h, 0:1, :] = total[0:1]
-        edge[h, 1:2, :] = jnp.broadcast_to(jnp.sum(total[1 : 1 + patches, 0:1], 0, keepdims=True), (1, keys))
-        block = jnp.where(inner, total, 0.0)
+        block = jnp.where(lane > 0, total, 0.0)
         sums = None
         for r in range(grid):
             part = block[1 + r * grid : 1 + (r + 1) * grid]
             part = jnp.concatenate([part, jnp.zeros((grid, wide - keys), F32)], 1)
             part = pltpu.roll(part, (grid * (grid - 1 - r) - 1) % wide, 1)
             sums = part if sums is None else sums + part
-        by_col[h] = sums
+        tiles = [jnp.zeros((grid, 128), F32) for _ in range(out.shape[1] // 128 + 1)]
+        for a in range(side):
+            at, to = a * side // 128, a * grid // 128 * 128
+            start = a * grid - to
+            inside = (narrow >= start) & (narrow < start + grid)
+            window = jnp.where(inside, sums[:, to : to + 256], 0.0)
+            turned = pltpu.roll(window, (a * side + grid - 1 - at * 128 - start) % 256, 1)
+            tiles[at] = tiles[at] + turned[:, :128]
+            tiles[at + 1] = tiles[at + 1] + turned[:, 128:]
+        slid = jnp.concatenate(tiles[:-1], 1)
+        flat = slid[0:1]
+        for c in range(1, grid):
+            flat = flat + pltpu.roll(slid[c : c + 1], out.shape[1] - c, 1)
+        upper = jnp.sum(jnp.where(lane > 0, total[0:1], 0.0), 1, keepdims=True)
+        left = jnp.sum(total[1 : 1 + patches, 0:1], 0, keepdims=True)
+        for k, value in enumerate((upper, left, total[0:1, 0:1])):
+            flat = jnp.where(last == side * side + k, value, flat)
+        out[h : h + 1, :] = flat
 
 
 def place_sums(refs_in, refs_out, scratch):
@@ -392,18 +438,31 @@
     cp.finish()
 
 
-def bias_fill(grid, tail, by_col, out):
+def bias_fill(grid, tail, flipped, out):
     heads, rows, keys = out.shape
-    patches = grid * grid
-    wide = by_col.shape[2]
+    patches, side = grid * grid, 2 * grid - 1
+    wide = -(-(side * grid) // 128) * 128
+    high = -(-grid // 8) * 8
     lane = lax.broadcasted_iota(jnp.int32, (1, keys), 1)
+    narrow = lax.broadcasted_iota(jnp.int32, (1, 128), 1)
     for h in range(heads):
         corner, upper, left = tail[h, 2], tail[h, 0], tail[h, 1]
         out[h, patches + 1 :, :] = jnp.where(
             lax.broadcasted_iota(jnp.int32, (rows - patches - 1, keys), 1) <= patches, 0.0, -1e30
         )
         out[h, 0:1, :] = jnp.where(lane == 0, corner, jnp.where(lane <= patches, upper, -1e30))
-        block = by_col[h]
+        slid = jnp.broadcast_to(flipped[h : h + 1, :], (high, flipped.shape[1]))
+        slid = pltpu.roll(slid, 0, 1, stride=1, stride_axis=0)
+        tiles = [jnp.zeros((high, 128), F32) for _ in range(wide // 128)]
+        for a in range(side):
+            at, to = a * side // 128 * 128, a * grid // 128
+            start = a * grid - to * 128
+            turned = pltpu.roll(slid[:, at : at + 256], (start - (a * side + grid - 1 - at)) % 256, 1)
+            for k in range(2):
+                if 128 * k < start + grid and start < 128 * (k + 1):
+                    inside = (narrow >= start - 128 * k) & (narrow < start + grid - 128 * k)
+                    tiles[to + k] = jnp.where(inside, turned[:, 128 * k : 128 * (k + 1)], tiles[to + k])
+        block = jnp.concatenate(tiles, 1)
         for r in range(grid):
             turned = pltpu.roll(block, (1 - grid * (grid - 1 - r)) % wide, 1)[0:grid, 0:keys]
             turned = jnp.where(lane == 0, left, jnp.where(lane <= patches, turned, -1e30))
@@ -460,30 +519,24 @@
     def __init__(self, images, rows, keys, width, hidden, heads):
         self.n, self.r, self.k, self.d, self.f, self.h = images, rows, keys, width, hidden, heads
 
-    def weights(self, flags, own, other, own_d, other_d):
-        d, f = self.d, self.f
-        return pl.pallas_call(
-            lambda *refs: load_weights(refs[:5], refs[5:8], refs[8:]),
-            out_shape=(pltpu.VMEM((d, f), BF), pltpu.VMEM((d, f), BF), pltpu.VMEM((f, d), BF)),
-            in_specs=[SMEM] + [ANY] * 4,
-            out_specs=(VMEM, VMEM, VMEM),
-            scratch_shapes=[pltpu.SemaphoreType.DMA((3,))],
-            compiler_params=pltpu.CompilerParams(vmem_limit_bytes=4 * 2**20),
-            name="load_weights",
-        )(flags, *[in_hbm(v) for v in (own, other, own_d, other_d)])
-
     def forward(self, i, flags, x, vec_a, vec_f, weights, bias, state):
         n, r, k, d, f, h = self.n, self.r, self.k, self.d, self.f, self.h
         narrow, wide = far((n, r, d)), far((n, r, f))
         held = pltpu.VMEM((n, r, d), BF)
-        shapes = [far((n, 5, r, d)), held, held, narrow, far((n, h, r, k)), pltpu.VMEM((n, r, f), BF), held, wide, narrow, narrow]
+        shapes = [far((n, 5, r, d)), held, held, narrow, far((n, h, r, k)), pltpu.VMEM((n, r, f), BF), held, wide, narrow, narrow, narrow]
         row, high = sd((r, d)), sd((r, f))
         scratch = [row, sd((k, 3 * d)), sd((h, r, k)), row, row, high, row, row]
-        ins = [flags, pinned(x), vec_a, vec_f, *[pinned(w) for w in weights], pinned(bias)]
+        ins, specs = [flags, pinned(x), vec_a, vec_f, pinned(bias)], [SMEM] + [VMEM] * 4
+        extra = [pltpu.VMEM((r, d), BF)]
+        if len(weights) > 3:
+            ins, specs = ins + list(weights), specs + [ANY] * 4
+            extra += [pltpu.VMEM((d, f), BF), pltpu.VMEM((d, f), BF), pltpu.VMEM((f, d), BF)]
+        else:
+            ins, specs = ins + [pinned(w) for w in weights], specs + [VMEM] * 3
         flops = 2 * r * d * 4 * d + 4 * h * r * k * HD + 4 * r * d * f
-        return run(forward_image, i, "forward_image", ins, [SMEM] + [VMEM] * 7, state, shapes, [pltpu.VMEM((r, d), BF)], scratch, 20, flops, 12000000)
-
-    def backward(self, i, flags, g, vec_a, vec_f, weights, kept, state):
+        return run(forward_image, i, "forward_image", ins, specs, state, shapes, extra, scratch, 20, flops, 12000000)
+
+    def backward(self, i, flags, g, vec_a, vec_f, weights, hide, kept, state):
         n, r, k, d, f, h = self.n, self.r, self.k, self.d, self.f, self.h
         narrow = far((n, r, d))
         sums = far((n, 8, d), F32)
@@ -491,13 +544,13 @@
         shapes = [pltpu.VMEM((n, r, f), BF), held, narrow, sums, held, pltpu.VMEM((n, r, 3 * d), BF), far((n, h, r, k)), narrow, sums]
         row, high, pairs, vec = sd((r, d)), sd((r, f)), sd((h, r, k)), sd((8, d), F32)
         scratch = [row, high, row, row, sd((k, 3 * d)), pairs, row, row, row, vec, row, pairs, row, vec]
-        sa, a1, ctx, y1, pb, g_all, a2, gp, b2, y2 = kept
-        ins = [flags, pinned(g), vec_a, vec_f, *[pinned(w) for w in weights], sa, pb, y1, gp, b2]
+        sa, a1, ctx, y1, pb, g_all, a2, gp, b2 = kept[:9]
+        ins = [flags, pinned(g), vec_a, vec_f, *[pinned(w) for w in weights], hide, sa, pb, y1, gp, b2]
         flops = 2 * r * d * 4 * d + 8 * h * r * k * HD + 4 * r * d * f
-        return run(backward_image, i, "backward_image", ins, [SMEM] + [VMEM] * 6 + [ANY] * 5, state, shapes, [pltpu.VMEM((r, d), BF)], scratch, 24, flops, 12000000)
+        return run(backward_image, i, "backward_image", ins, [SMEM] + [VMEM] * 7 + [ANY] * 5, state, shapes, [pltpu.VMEM((r, d), BF)], scratch, 24, flops, 12000000)
 
     def parts(self, ups, flags, blocks, chunks):
-        d = self.d
+        n, r, d = self.n, self.r, self.d
         tall = d // chunks
         both = (chunks, tall + tall // 2, d)
         made = pl.pallas_call(
@@ -506,34 +559,40 @@
             in_specs=[SMEM] + [VMEM] * 8,
             out_specs=(ANY,) * 8,
             scratch_shapes=[pltpu.VMEM((2, *both), BF)] * 2 + [pltpu.SemaphoreType.DMA((8 * chunks,))],
-            compiler_params=pltpu.CompilerParams(vmem_limit_bytes=28 * 2**20),
-            cost_estimate=pl.CostEstimate(flops=1, bytes_accessed=1, transcendentals=0),
+            compiler_params=pltpu.CompilerParams(vmem_limit_bytes=16 * 2**20),
+            cost_estimate=pl.CostEstimate(flops=24 * n * r * d * d, bytes_accessed=14000000, transcendentals=0),
             name="weight_parts",
         )(flags, *[pinned(v) for v in blocks])
         return made[:4], made[4:]
 
+    def join(self, flags, keep, got, length, dtype):
+        n, r, d = keep.shape
+        return pl.pallas_call(
+            lambda *refs: join_images(refs[:3], refs[3], refs[4:]),
+            out_shape=sd((length, 2 * n, d), dtype),
+            in_specs=[SMEM] + [ANY] * 2,
+            out_specs=VMEM,
+            scratch_shapes=[pltpu.VMEM((2 * n, r, d), BF), pltpu.SemaphoreType.DMA((2,))],
+            compiler_params=pltpu.CompilerParams(vmem_limit_bytes=16 * 2**20),
+            cost_estimate=pl.CostEstimate(flops=0, bytes_accessed=10000000, transcendentals=0),
+            name="join_images",
+        )(flags, in_hbm(keep), in_hbm(got))
+
     def table(self, dl, grid):
         n, heads, rows, keys = dl.shape
         side = 2 * grid - 1
-        wide = -(-(side * grid) // 128) * 128
-        by_col, edge = pl.pallas_call(
+        wide = -(-(side * side + 3 + grid) // 128) * 128
+        flat = pl.pallas_call(
             partial(table_fold, grid),
-            out_shape=(sd((heads, grid, wide), F32), sd((heads, 2, keys), F32)),
+            out_shape=sd((heads, wide), F32),
             in_specs=[ANY],
-            out_specs=(VMEM, VMEM),
+            out_specs=VMEM,
             scratch_shapes=[pltpu.VMEM((heads, n, rows, keys), BF), pltpu.SemaphoreType.DMA((heads,))],
-            compiler_params=pltpu.CompilerParams(vmem_limit_bytes=24 * 2**20),
+            compiler_params=pltpu.CompilerParams(vmem_limit_bytes=16 * 2**20),
+            cost_estimate=pl.CostEstimate(flops=0, bytes_accessed=8000000, transcendentals=0),
             name="table_fold",
         )(in_hbm(dl))
-        by_col = by_col[:, :, : side * grid].reshape(heads, grid, side, grid)
-        flipped = 0.0
-        for c in range(grid):
-            at = grid - 1 - c
-            flipped = flipped + jnp.pad(by_col[:, c], ((0, 0), (0, 0), (at, side - at - grid)))
-        inner = flipped[:, ::-1, ::-1].reshape(heads, side * side)
-        patches = grid * grid
-        tail = jnp.stack([jnp.sum(edge[:, 0, 1 : 1 + patches], 1), edge[:, 1, 0], edge[:, 0, 0]], 1)
-        return jnp.concatenate([inner, tail], 1)
+        return flat
 
     def place(self, flags, a_up, a_down, b_up, b_down, state):
         d, f = self.d, self.f
@@ -547,27 +606,24 @@
             out_specs=(ANY, ANY),
             scratch_shapes=scratch,
             input_output_aliases={5: 0, 6: 1} if given else {},
-            compiler_params=pltpu.CompilerParams(vmem_limit_bytes=24 * 2**20),
-            cost_estimate=pl.CostEstimate(flops=0, bytes_accessed=1, transcendentals=0),
+            compiler_params=pltpu.CompilerParams(vmem_limit_bytes=16 * 2**20),
+            cost_estimate=pl.CostEstimate(flops=0, bytes_accessed=4000000, transcendentals=0),
             name="place_sums",
         )(flags, a_up, a_down, b_up, b_down, *(() if state is None else state))
 
     def bias(self, table, grid):
         heads = table.shape[0]
         side = 2 * grid - 1
-        flipped = table[:, : side * side].reshape(heads, side, side)[:, ::-1, ::-1]
-        by_col = jnp.stack([flipped[:, :, grid - 1 - c : side - c] for c in range(grid)], 1)
-        by_col = by_col.reshape(heads, grid, side * grid)
-        wide = -(-(side * grid) // 128) * 128
-        by_col = jnp.pad(by_col, ((0, 0), (0, -grid % 8), (0, wide - side * grid)))
+        flipped = table[:, : side * side][:, ::-1]
+        flipped = jnp.pad(flipped, ((0, 0), (0, -side * side % 128 + 128)))
         return pl.pallas_call(
             partial(bias_fill, grid),
             out_shape=pltpu.VMEM((heads, self.r, self.k), F32),
             in_specs=[SMEM, VMEM],
             out_specs=VMEM,
-            compiler_params=pltpu.CompilerParams(vmem_limit_bytes=24 * 2**20),
+            compiler_params=pltpu.CompilerParams(vmem_limit_bytes=16 * 2**20),
             name="bias_fill",
-        )(table[:, side * side :], by_col)
+        )(table[:, side * side :], flipped)
 
 
 def swap(block, pairs):
@@ -578,29 +634,22 @@
     return list(range(0, n, 2)) + list(range(n - 1, 0, -2))
 
 
-def doubled_sum(block, axis):
-    n = lax.axis_size(axis)
-    step = 1
-    while step < n:
-        block = block + lax.ppermute(block, axis, [(k, k ^ step) for k in range(n)])
-        step *= 2
-    return block
-
-
-def weight_shares(kern, blocks, core, both):
+def ring_place():
     n = lax.axis_size("dp")
-    ringed = n == RING
     place = [0] * n
     for k, device in enumerate(ring_order(n)):
         place[device] = k
-    at = jnp.array(place, jnp.int32)[lax.axis_index("dp")] if ringed else jnp.int32(0)
-    flags = jnp.stack([core, at])
+    return jnp.array(place, jnp.int32)[lax.axis_index("dp")] if n == RING else jnp.int32(0)
+
+
+def weight_shares(kern, flags, blocks, both):
+    ringed = lax.axis_size("dp") == RING
     sents, owns = kern.parts([ringed, ringed, False, False], flags, blocks, RING)
     got = {s: swap(sents[s], both) for s in (0, 2, 1, 3)}
-    return [(owns[s], got[s]) for s in range(4)], at
-
-
-def weight_sums(kern, locals_, at, small, low, core, to_low, to_high, sections):
+    return [(owns[s], got[s]) for s in range(4)]
+
+
+def weight_sums(kern, locals_, at, carry, tasks, low, core, to_low, to_high, sections):
     axis = "dp"
     n = lax.axis_size(axis)
     ringed = n == RING
@@ -616,7 +665,11 @@
         columns = jnp.where(low, kept, got_first).transpose(1, 2, 0, 3)
         grad_weight = columns.reshape(kern.d, kern.f).astype(F32)
         grad_down = jnp.where(low, 0.0, first.astype(F32)).reshape(kern.f, kern.d)
-        return grad_weight, grad_down, doubled_sum(small, axis)
+        for task in tasks:
+            carry, waiting = task(carry)
+            if waiting is not None:
+                carry = {**carry, **waiting}
+        return grad_weight, grad_down, carry
 
     route = {w: [(order[k], order[(k + w) % n]) for k in range(n)] for w in (1, -1)}
     upper = {
@@ -636,22 +689,22 @@
     kept = jnp.where(low, jnp.concatenate([second, got_second], 1), first)
     a = {1: kept[:2], -1: kept[2:]}
     b = {1: got_first[:2], -1: got_first[2:]}
+    a, b, carry = lax.optimization_barrier((a, b, carry))
     state = None
-    step, other = 1, None
     for k in range(n):
         index = jnp.stack([core, (at + 1 - k) & (n - 1), (at - 1 + k) & (n - 1)])
         if k < n - 1:
             next_a = {w: lax.ppermute(a[w], axis, route[w]) for w in (1, -1)}
             next_b = {w: lax.ppermute(b[w], ("section", axis), upper[w]) for w in (1, -1)}
         state = kern.place(index, a[1], a[-1], b[1], b[-1], state)
+        waiting = None
+        if k < len(tasks):
+            carry, waiting = tasks[k](carry)
         if k < n - 1:
-            if k % 2 == 0 and step < n:
-                other = lax.ppermute(small, axis, [(d, d ^ step) for d in range(n)])
-                step *= 2
-            if k % 2 == 1 and other is not None:
-                small, other = small + other, None
-            a, b, state, small = lax.optimization_barrier((next_a, next_b, state, small))
-    return (*state, small)
+            a, b, state, carry = lax.optimization_barrier((next_a, next_b, state, carry))
+        if waiting is not None:
+            carry = {**carry, **waiting}
+    return (*state, carry)
 
 
 def on_device(embeds, mask, cotangent, section_weight, down_weight, section_vectors, rel_table):
@@ -685,19 +738,24 @@
     start = jnp.where(cover, vec_a[6].astype(BF), mine_of(embeds))
     pad = ((0, 0), (0, rows - length), (0, 0))
     start = jnp.pad(start, pad)
+    hide = jnp.pad((cover & (stage == 0)).astype(F32), pad)
     upstream = jnp.pad(mine_of(cotangent), pad)
 
     kern = Kernels(half, rows, keys, width, hidden, heads)
+    at = ring_place()
+    flags_p = jnp.stack([core, at])
+    table, flags_p, at = lax.optimization_barrier((table, flags_p, at))
     bias = kern.bias(table, grid)
     flags_a = jnp.stack([(stage == 0).astype(jnp.int32), core])
     flags_b = jnp.stack([(stage == 1).astype(jnp.int32), core])
-    weights = kern.weights(flags_a, own_w, other_w, own_d, other_d)
+    weights = [own_w, other_w, own_d, other_d]
     kept, grads = None, None
 
     def forward(i, flags, x):
-        nonlocal kept
-        kept, (send,) = kern.forward(i, flags, x, vec_a, vec_f, weights, bias, kept)
-        return send
+        nonlocal kept, weights
+        kept, made = kern.forward(i, flags, x, vec_a, vec_f, weights, bias, kept)
+        weights = made[1:] or weights
+        return made[0]
 
     arrived = [swap(forward(i, flags_a, start), onward) for i in range(half)]
     for i in range(half):
@@ -705,56 +763,87 @@
 
     def backward(i, flags, g):
         nonlocal grads
-        grads, (send,) = kern.backward(i, flags, g, vec_a, vec_f, weights, kept, grads)
+        grads, (send,) = kern.backward(i, flags, g, vec_a, vec_f, weights, hide, kept, grads)
         return send
 
     returned = [swap(backward(i, flags_b, upstream), back) for i in range(half)]
     for i in range(half):
         backward(i, flags_a, returned[i])
 
-    sa, a1, ctx, y1, pb, g_all, a2, gp, b2, y2 = kept
-    dh_all, ef, dx1, vgf, ea, dq, dl, dx0, vga = grads
-    shares, at = weight_shares(kern, (g_all, dh_all, a2, ef, a1, ctx, dq, ea), core, both)
-    own_parts, vga, vgf, dl, dx0, dx1 = lax.optimization_barrier(([v[0] for v in shares], vga, vgf, dl, dx0, dx1))
+    sa, a1, ctx, y1, pb, g_all, a2, gp, b2, keep_y, give_y = kept
+    dh_all, ef, keep_x, vgf, ea, dq, dl, give_x, vga = grads
+    blocks = (g_all, dh_all, a2, ef, a1, ctx, dq, ea)
+    shares = weight_shares(kern, flags_p, blocks, both)
+    own_parts, vga, vgf, dl, keep_x, give_x, keep_y, give_y = lax.optimization_barrier(
+        ([v[0] for v in shares], vga, vgf, dl, keep_x, give_x, keep_y, give_y)
+    )
     shares = [(own, other) for own, (_, other) in zip(own_parts, shares)]
-    rows_a = jnp.sum(vga, 0)
-    token = jnp.sum(jnp.where(cover, dx0[:, :length].astype(F32), 0.0), (0, 1))
-    rows_a = rows_a.at[6].add(jnp.where(stage == 0, token, 0.0))
-    rows_f = jnp.sum(vgf, 0)
-    row_terms = jnp.where(low, rows_a, rows_f) + swap(jnp.where(low, rows_f, rows_a), both)
-    sums = kern.table(dl, grid) * (HD ** 0.5)
-    sums = jnp.where(low, sums + swap(sums, to_low), 0.0)
-    entries = sums.shape[1]
-    wide = -(-entries // 128) * 128
-    small = jnp.concatenate([row_terms.reshape(-1), jnp.pad(sums, ((0, 0), (0, wide - entries))).reshape(-1)])
-    grad_weight, grad_down, small = weight_sums(
+    dp = lax.axis_size("dp")
+
+    def mine_and_theirs(a_part, f_part):
+        return jnp.where(low, a_part, f_part), jnp.where(low, f_part, a_part)
+
+    def vector_sums(carry):
+        return mine_and_theirs(jnp.sum(carry["vga"], 0), jnp.sum(carry["vgf"], 0))
+
+    def rest(carry, *used):
+        return {k: v for k, v in carry.items() if k not in used}
+
+    def swap_y(carry):
+        return rest(carry, "give_y"), {"got_y": swap(carry["give_y"], both)}
+
+    def start_sums(carry):
+        mine, theirs = vector_sums(carry)
+        sums = kern.table(carry["dl"], grid)
+        flat = jnp.concatenate([jnp.where(low, sums, 0.0).reshape(-1, 128), mine.reshape(-1, 128)])
+        away = jnp.concatenate([jnp.where(low, 0.0, sums).reshape(-1, 128), theirs.reshape(-1, 128)])
+        return {"small": flat, **rest(carry, "dl", "vga", "vgf")}, {"got": swap(away, both)}
+
+    def doubling(step):
+        def task(carry):
+            small = carry["small"] + carry["got"]
+            got = lax.ppermute(small, "dp", [(d, d ^ step) for d in range(dp)])
+            return {**rest(carry, "got"), "small": small}, {"got": got}
+
+        return task
+
+    def join_y(carry):
+        joined = kern.join(flags_a[1:], carry["keep_y"], carry["got_y"], length, BF)
+        return {"y": joined, **rest(carry, "keep_y", "got_y", "give_x")}, {"got_x": swap(carry["give_x"], both)}
+
+    def join_x(carry):
+        joined = kern.join(flags_a[1:], carry["keep_x"], carry["got_x"], length, F32)
+        return {"x": joined, **rest(carry, "keep_x", "got_x")}, None
+
+    steps = [doubling(1 << k) for k in range(dp.bit_length() - 1)]
+    tasks = [swap_y, start_sums, join_y, steps[0], join_x, *steps[1:]]
+    grad_weight, grad_down, carry = weight_sums(
         kern,
         shares,
         at,
-        small.reshape(-1, 128),
-        low, core, to_low, to_high, sections
+        {"dl": dl, "vga": vga, "vgf": vgf, "keep_y": keep_y, "give_y": give_y, "keep_x": keep_x, "give_x": give_x},
+        tasks,
+        low,
+        core,
+        to_low,
+        to_high,
+        sections,
     )
-
-    small = small.reshape(-1)
-    grad_rows = small[: 8 * width].reshape(8, width)
-    grad_table = small[8 * width :].reshape(heads, wide)[:, :entries]
-
-    def gather_images(a_part, f_part):
-        mine, theirs = jnp.where(low, a_part, f_part), jnp.where(low, f_part, a_part)
-        got = swap(theirs, both)
-        return jnp.concatenate([jnp.where(low, mine, got), jnp.where(low, got, mine)], 0)[:, :length]
-
-    activations = gather_images(y1, y2)
-    input_grads = gather_images(dx0, dx1).astype(F32)
-    hide = (mask[:, :, None] == 1) & (now == 0)
-    input_grads = jnp.where(hide, 0.0, input_grads)
+    small = carry["small"] + carry["got"]
+    cut = small.shape[0] - 8 * width // 128
+    grad_rows = small[cut:].reshape(8, width)
+    flat = small[:cut].reshape(heads, -1)[:, : own_t.shape[1]] * (HD ** 0.5)
+    pairs = own_t.shape[1] - 3
+    grad_table = jnp.concatenate([flat[:, :pairs][:, ::-1], flat[:, pairs:]], 1)
+    activations = carry["y"].transpose(1, 0, 2)
+    input_grads = carry["x"].transpose(1, 0, 2)
     return (
         activations[None],
         input_grads[None],
         grad_weight[None],
         grad_down[None],
         grad_rows[None],
-        grad_table[None],
+        jnp.where(low, grad_table, 0.0)[None],
     )
 
 

time: 419 us -> 398 us (0.950)
  other arithmetic: 36.8 us -> 10.5 us
  local copies, waits for them, and re-layouts: 29.2 us -> 11.2 us
  waiting for transfers between devices: 45.1 us -> 62.4 us
    convert_element_type x32, other arithmetic: 25.4 us -> 7.25 us  [weight_sums(): held[s] = total.astype(BF)]
    ppermute x28, waiting for transfers between devices: 23.2 us -> 34.4 us  [weight_sums(): lax.ppermute(held[s], axis, route[1 if s < 2 else -1]).astype(F32)]
    ppermute x28, starting transfers between devices: 23 us -> 30.9 us  [weight_sums(): lax.ppermute(held[s], axis, route[1 if s < 2 else -1]).astype(F32)]
    ppermute x22 -> x21, waiting for transfers between devices: 6.4 us -> 14.1 us  [swap(): return lax.ppermute(block, 'section', pairs)]
    ppermute x22 -> x21, starting transfers between devices: 32.5 us -> 24.9 us  [swap(): return lax.ppermute(block, 'section', pairs)]
    pallas_call x2 -> x3, Pallas kernels: 8.81 us -> 15.7 us  [the longest x2 9.07 us: join(): pl.pallas_call(lambda *refs: join_images(refs[:3], refs[3], refs[4:]), ou...]
    select_n x7 -> x3, other arithmetic: 5.64 us -> 0.72 us  [the longest x1 0.7 us: on_device(): jnp.where(low, grad_table, 0.0)[None]]
    reshape x6 -> x3, local copies, waits for them, and re-layouts: 4.46 us -> 0.02 us  [the longest x1 0.01 us: on_device(): flat = small[:cut].reshape(heads, -1)[:, :own_t.shape[1]] * HD ** 0.5]
  transfers between devices with their start and end apart: 81 -> 80, of which waited for: 30 -> 36; matrix products, arithmetic and copies ran while one was open for 16% -> 4% of each run, Pallas kernels for 29% -> 33%
where the time goes in v1:
time: 398 us; the launch traced here: 391 us
  Pallas kernels  186 us (47%)
  starting transfers between devices  110 us (28%)
  waiting for transfers between devices  62.4 us (16%)
  local copies, waits for them, and re-layouts  11.2 us (3%)
  between operations  11.1 us (3%)
  other arithmetic  10.5 us (3%)
    pallas_call x16, Pallas kernels, run(): pl.pallas_call(kernel, out_shape=tuple(shapes) + tuple(extra), in_specs=l...  129 us
    ppermute x14, starting transfers between devices, weight_sums(): lax.ppermute(b[w], ('section', axis), upper[w])  37.2 us
    ppermute x28, waiting for transfers between devices, weight_sums(): lax.ppermute(held[s], axis, route[1 if s < 2 else -1]).astype(F32)  34.4 us
    ppermute x28, starting transfers between devices, weight_sums(): lax.ppermute(held[s], axis, route[1 if s < 2 else -1]).astype(F32)  30.9 us
    ppermute x21, starting transfers between devices, swap(): return lax.ppermute(block, 'section', pairs)  24.9 us
    pallas_call x1, Pallas kernels, parts(): pl.pallas_call(lambda *refs: weight_parts(ups, refs[:9], refs[9:13], refs...  20.3 us
    pallas_call x8, Pallas kernels, place(): pl.pallas_call(lambda *refs: place_sums(refs[:5], refs[5 + given:7 + give...  16.3 us
    ppermute x21, waiting for transfers between devices, swap(): return lax.ppermute(block, 'section', pairs)  14.1 us
  transfers between devices with their start and end apart: 80, of which 36 were waited for; matrix products, arithmetic and copies ran while one was open for 4% of the time, Pallas kernels for 33%

profile of v1, /device:TPU:1, one launch (start us, length us, event | category | flops | bytes accessed | tf_op | source)
XLA Modules:
  0.0 391.2 jit_solution(9704445418136151929)
XLA Ops:
  0.8 4.5 %collective-permute-start.3 = (bf16[3072,768]{1,0:T(8,128)(2,1)}, bf16[3072,768]{1,0:T(8,128)(2,1)}, u32[]{:S(2)}, u32[]{:S(2)}) collective-permute-start(bf16[3072,768]{1,0:T(8,128)(2,1)} %bitcast.184), channel_id=1, source_target_pairs={{8,0},{24,16},{9,1},{25,17},{10,2},{26,18},{11,3},{27,19},{12,4},{... | collective-permute-start | bytes 14155784 | tf_op jit(solution)/shard_map/ppermute | solution.py:630
  10.5 4.7 %constant_dynamic-slice_fusion = (bf16[4,197,768]{2,0,1:T(4,128)(2,1)S(1)}, bf16[4,197,768]{2,0,1:T(4,128)(2,1)}) fusion(bf16[8,197,768]{2,0,1:T(8,128)(2,1)} %param.10, s32[]{:T(128)S(6)} %select_n.102, bf16[8,197,768]{2,0,1:T(8,128)(2,1)} %param.8), kind=kLoop, calls=%fused_computation.94 | loop fusion | bytes 4841476 | tf_op jit(solution)/shard_map/dynamic_slice | solution.py:735
  18.3 4.9 %bias_fill.1.refs_4_ = f32[12,208,256]{2,1,0:T(8,128)S(1)} custom-call(f32[12,3]{1,0:T(8,128)S(1)} %slice.254.tail, f32[12,896]{1,0:T(8,128)S(1)} %pad.18.flipped), custom_call_target="tpu_custom_call" | custom-call | tf_op jit(solution)/shard_map/bias_fill/pallas_call | solution.py:619
  23.2 11.7 %forward_image.8 = (bf16[4,5,208,768]{3,2,1,0:T(8,128)(2,1)}, bf16[4,208,768]{2,1,0:T(8,128)(2,1)S(1)}, bf16[4,208,768]{2,1,0:T(8,128)(2,1)S(1)}, bf16[4,208,768...) custom-call(s32[2]{0:T(128)S(1)} %pad_add_fusion.2.refs_0_, ...), custom_call_target="tpu_custom_call" | custom-call | flops 3107979264 | bytes 12000000 | tf_op jit(solution)/shard_map/forward_image/pallas_call | solution.py:484
  36.2 10.7 %forward_image.9 = (bf16[4,5,208,768]{3,2,1,0:T(8,128)(2,1)}, bf16[4,208,768]{2,1,0:T(8,128)(2,1)S(1)}, bf16[4,208,768]{2,1,0:T(8,128)(2,1)S(1)}, bf16[4,208,768...) custom-call(s32[2]{0:T(128)S(1)} %pad_add_fusion.2.refs_0_, ...), custom_call_target="tpu_custom_call", output_to_operand_aliasing={{0}: (8, {}), {1}: (9, {}), {2}: (10, {}), {3}: (11, {}), {... | custom-call | flops 3107979264 | bytes 12000000 | tf_op jit(solution)/shard_map/forward_image/pallas_call | solution.py:484
  48.2 10.4 %forward_image.10 = (bf16[4,5,208,768]{3,2,1,0:T(8,128)(2,1)}, bf16[4,208,768]{2,1,0:T(8,128)(2,1)S(1)}, bf16[4,208,768]{2,1,0:T(8,128)(2,1)S(1)}, bf16[4,208,76...) custom-call(s32[2]{0:T(128)S(1)} %pad_add_fusion.2.refs_0_, ...), custom_call_target="tpu_custom_call", output_to_operand_aliasing={{0}: (8, {}), {1}: (9, {}), {2}: (10, {}), {3}: (11, {}), {... | custom-call | flops 3107979264 | bytes 12000000 | tf_op jit(solution)/shard_map/forward_image/pallas_call | solution.py:484
  59.9 10.4 %forward_image.11 = (bf16[4,5,208,768]{3,2,1,0:T(8,128)(2,1)}, bf16[4,208,768]{2,1,0:T(8,128)(2,1)S(1)}, bf16[4,208,768]{2,1,0:T(8,128)(2,1)S(1)}, bf16[4,208,76...) custom-call(s32[2]{0:T(128)S(1)} %pad_add_fusion.2.refs_0_, ...), custom_call_target="tpu_custom_call", output_to_operand_aliasing={{0}: (8, {}), {1}: (9, {}), {2}: (10, {}), {3}: (11, {}), {... | custom-call | flops 3107979264 | bytes 12000000 | tf_op jit(solution)/shard_map/forward_image/pallas_call | solution.py:484
  73.4 5.0 %forward_image.13 = (bf16[4,5,208,768]{3,2,1,0:T(8,128)(2,1)}, bf16[4,208,768]{2,1,0:T(8,128)(2,1)S(1)}, bf16[4,208,768]{2,1,0:T(8,128)(2,1)S(1)}, bf16[4,208,76...) custom-call(s32[2]{0:T(128)S(1)} %pad_add_fusion.1.refs_0_, ...), custom_call_target="tpu_custom_call", output_to_operand_aliasing={{0}: (8, {}), {1}: (9, {}), {2}: (10, {}), {3}: (11, {}), {... | custom-call | flops 3107979264 | bytes 12000000 | tf_op jit(solution)/shard_map/forward_image/pallas_call | solution.py:484
  78.4 5.2 %forward_image.14 = (bf16[4,5,208,768]{3,2,1,0:T(8,128)(2,1)}, bf16[4,208,768]{2,1,0:T(8,128)(2,1)S(1)}, bf16[4,208,768]{2,1,0:T(8,128)(2,1)S(1)}, bf16[4,208,76...) custom-call(s32[2]{0:T(128)S(1)} %pad_add_fusion.1.refs_0_, ...), custom_call_target="tpu_custom_call", output_to_operand_aliasing={{0}: (8, {}), {1}: (9, {}), {2}: (10, {}), {3}: (11, {}), {... | custom-call | flops 3107979264 | bytes 12000000 | tf_op jit(solution)/shard_map/forward_image/pallas_call | solution.py:484
  83.6 4.8 %forward_image.15 = (bf16[4,5,208,768]{3,2,1,0:T(8,128)(2,1)}, bf16[4,208,768]{2,1,0:T(8,128)(2,1)S(1)}, bf16[4,208,768]{2,1,0:T(8,128)(2,1)S(1)}, bf16[4,208,76...) custom-call(s32[2]{0:T(128)S(1)} %pad_add_fusion.1.refs_0_, ...), custom_call_target="tpu_custom_call", output_to_operand_aliasing={{0}: (8, {}), {1}: (9, {}), {2}: (10, {}), {3}: (11, {}), {... | custom-call | flops 3107979264 | bytes 12000000 | tf_op jit(solution)/shard_map/forward_image/pallas_call | solution.py:484
  88.4 4.7 %backward_image.8 = (bf16[4,208,3072]{2,1,0:T(8,128)(2,1)S(1)}, bf16[4,208,768]{2,1,0:T(8,128)(2,1)S(1)}, bf16[4,208,768]{2,1,0:T(8,128)(2,1)}, f32[4,8,768]{2,1...) custom-call(s32[2]{0:T(128)S(1)} %pad_add_fusion.1.refs_0_, ...), custom_call_target="tpu_custom_call" | custom-call | flops 3271557120 | bytes 12000000 | tf_op jit(solution)/shard_map/backward_image/pallas_call | solution.py:484
  94.5 4.1 %backward_image.9 = (bf16[4,208,3072]{2,1,0:T(8,128)(2,1)S(1)}, bf16[4,208,768]{2,1,0:T(8,128)(2,1)S(1)}, bf16[4,208,768]{2,1,0:T(8,128)(2,1)}, f32[4,8,768]{2,1...) custom-call(s32[2]{0:T(128)S(1)} %pad_add_fusion.1.refs_0_, ...), custom_call_target="tpu_custom_call", output_to_operand_aliasing={{0}: (13, {}), {1}: (14, {}), {2}: (15, {}), {3}: (16, {}),... | custom-call | flops 3271557120 | bytes 12000000 | tf_op jit(solution)/shard_map/backward_image/pallas_call | solution.py:484
  99.9 4.2 %backward_image.10 = (bf16[4,208,3072]{2,1,0:T(8,128)(2,1)S(1)}, bf16[4,208,768]{2,1,0:T(8,128)(2,1)S(1)}, bf16[4,208,768]{2,1,0:T(8,128)(2,1)}, f32[4,8,768]{2,...) custom-call(s32[2]{0:T(128)S(1)} %pad_add_fusion.1.refs_0_, ...), custom_call_target="tpu_custom_call", output_to_operand_aliasing={{0}: (13, {}), {1}: (14, {}), {2}: (15, {}), {3}: (16, {}),... | custom-call | flops 3271557120 | bytes 12000000 | tf_op jit(solution)/shard_map/backward_image/pallas_call | solution.py:484
  105.4 4.4 %backward_image.11 = (bf16[4,208,3072]{2,1,0:T(8,128)(2,1)S(1)}, bf16[4,208,768]{2,1,0:T(8,128)(2,1)S(1)}, bf16[4,208,768]{2,1,0:T(8,128)(2,1)}, f32[4,8,768]{2,...) custom-call(s32[2]{0:T(128)S(1)} %pad_add_fusion.1.refs_0_, ...), custom_call_target="tpu_custom_call", output_to_operand_aliasing={{0}: (13, {}), {1}: (14, {}), {2}: (15, {}), {3}: (16, {}),... | custom-call | flops 3271557120 | bytes 12000000 | tf_op jit(solution)/shard_map/backward_image/pallas_call | solution.py:484
  111.2 4.4 %collective-permute-done.11.refs_1_ = bf16[208,768]{1,0:T(8,128)(2,1)S(1)} collective-permute-done((bf16[208,768]{1,0:T(8,128)(2,1)S(1)}, bf16[208,768]{1,0:T(8,128)(2,1)S(1)}, u32[]{:S(2)}, u32[]{:S(2)}) %collective-permute-start.11) | collective-permute-done | bytes 319520 | tf_op jit(solution)/shard_map/ppermute | solution.py:630
  115.6 12.8 %backward_image.12 = (bf16[4,208,3072]{2,1,0:T(8,128)(2,1)S(1)}, bf16[4,208,768]{2,1,0:T(8,128)(2,1)S(1)}, bf16[4,208,768]{2,1,0:T(8,128)(2,1)}, f32[4,8,768]{2,...) custom-call(s32[2]{0:T(128)S(1)} %pad_add_fusion.2.refs_0_, ...), custom_call_target="tpu_custom_call", output_to_operand_aliasing={{0}: (13, {}), {1}: (14, {}), {2}: (15, {}), {3}: (16, {}),... | custom-call | flops 3271557120 | bytes 12000000 | tf_op jit(solution)/shard_map/backward_image/pallas_call | solution.py:484
  129.1 12.9 %backward_image.13 = (bf16[4,208,3072]{2,1,0:T(8,128)(2,1)S(1)}, bf16[4,208,768]{2,1,0:T(8,128)(2,1)S(1)}, bf16[4,208,768]{2,1,0:T(8,128)(2,1)}, f32[4,8,768]{2,...) custom-call(s32[2]{0:T(128)S(1)} %pad_add_fusion.2.refs_0_, ...), custom_call_target="tpu_custom_call", output_to_operand_aliasing={{0}: (13, {}), {1}: (14, {}), {2}: (15, {}), {3}: (16, {}),... | custom-call | flops 3271557120 | bytes 12000000 | tf_op jit(solution)/shard_map/backward_image/pallas_call | solution.py:484
  142.7 12.9 %backward_image.14 = (bf16[4,208,3072]{2,1,0:T(8,128)(2,1)S(1)}, bf16[4,208,768]{2,1,0:T(8,128)(2,1)S(1)}, bf16[4,208,768]{2,1,0:T(8,128)(2,1)}, f32[4,8,768]{2,...) custom-call(s32[2]{0:T(128)S(1)} %pad_add_fusion.2.refs_0_, ...), custom_call_target="tpu_custom_call", output_to_operand_aliasing={{0}: (13, {}), {1}: (14, {}), {2}: (15, {}), {3}: (16, {}),... | custom-call | flops 3271557120 | bytes 12000000 | tf_op jit(solution)/shard_map/backward_image/pallas_call | solution.py:484
  156.6 13.1 %backward_image.15 = (bf16[4,208,3072]{2,1,0:T(8,128)(2,1)S(1)}, bf16[4,208,768]{2,1,0:T(8,128)(2,1)S(1)}, bf16[4,208,768]{2,1,0:T(8,128)(2,1)}, f32[4,8,768]{2,...) custom-call(s32[2]{0:T(128)S(1)} %pad_add_fusion.2.refs_0_, ...), custom_call_target="tpu_custom_call", output_to_operand_aliasing={{0}: (13, {}), {1}: (14, {}), {2}: (15, {}), {3}: (16, {}),... | custom-call | flops 3271557120 | bytes 12000000 | tf_op jit(solution)/shard_map/backward_image/pallas_call | solution.py:484
  169.7 20.3 %weight_parts.1 = (bf16[8,144,768]{2,1,0:T(8,128)(2,1)}, bf16[8,144,768]{2,1,0:T(8,128)(2,1)}, bf16[8,144,768]{2,1,0:T(8,128)(2,1)}, bf16[8,144,768]{2,1,0:T(8,1...) custom-call(s32[2]{0:T(128)S(1)} %pad_add_fusion.refs_0_, ...), custom_call_target="tpu_custom_call" | custom-call | flops 11777605632 | bytes 14000000 | tf_op jit(solution)/shard_map/weight_parts/pallas_call | solution.py:556
  264.2 4.6 %collective-permute-done.43 = bf16[144,768]{1,0:T(8,128)(2,1)S(1)} collective-permute-done((bf16[144,768]{1,0:T(8,128)(2,1)S(1)}, bf16[144,768]{1,0:T(8,128)(2,1)S(1)}, u32[]{:S(2)}, u32[]{:S(2)}) %collective-permute-start.43) | collective-permute-done | bytes 221216 | tf_op jit(solution)/shard_map/ppermute | solution.py:684
  269.0 4.1 %collective-permute-start.44 = (bf16[4,48,768]{2,1,0:T(8,128)(2,1)S(1)}, bf16[4,48,768]{2,1,0:T(8,128)(2,1)S(1)}, u32[]{:S(2)}, u32[]{:S(2)}) collective-permute-start(bf16[4,48,768]{2,1,0:T(8,128)(2,1)S(1)} %pad_maximum_fusion.1), channel_id=1, source_target_pairs={{8,0},{24,16},{9,1},{25,17},{10,2},{26,18},{11,3},{27,19},{12,4},{... | collective-permute-start | bytes 884744 | tf_op jit(solution)/shard_map/ppermute | solution.py:630
  291.8 6.6 %table_fold.1 = f32[12,768]{1,0:T(8,128)S(1)} custom-call(bf16[4,12,208,256]{3,2,1,0:T(8,128)(2,1)} %get-tuple-element.514.dl), custom_call_target="tpu_custom_call" | custom-call | bytes 8000000 | tf_op jit(solution)/shard_map/table_fold/pallas_call | solution.py:585
  300.0 3.2 collective-permute-start.52
  313.0 3.2 collective-permute-start.57
  319.8 4.2 %join_images.2 = bf16[197,8,768]{2,1,0:T(8,128)(2,1)} custom-call(s32[1]{0:T(128)} %bitcast.refs_0_, bf16[4,208,768]{2,1,0:T(8,128)(2,1)} %get-tuple-element.527.refs_1_, bf16[4,208,768]{2,1,0:T(8,128)(2,1)} %collective-permute-done.54.refs_2_), custom_call_target="tpu_custom_call" | custom-call | bytes 10000000 | tf_op jit(solution)/shard_map/join_images/pallas_call | solution.py:570
  327.6 3.2 collective-permute-start.62
  336.0 4.6 %collective-permute-done.63.refs_3_ = bf16[2,96,768]{2,1,0:T(8,128)(2,1)S(1)} collective-permute-done((bf16[2,96,768]{2,1,0:T(8,128)(2,1)S(1)}, bf16[2,96,768]{2,1,0:T(8,128)(2,1)S(1)}, u32[]{:S(2)}, u32[]{:S(2)}) %collective-permute-start.63) | collective-permute-done | bytes 294944 | tf_op jit(solution)/shard_map/ppermute | solution.py:698
  342.9 3.4 collective-permute-start.67
  352.5 4.9 %join_images.3 = f32[197,8,768]{2,1,0:T(8,128)} custom-call(s32[1]{0:T(128)} %bitcast.refs_0_, bf16[4,208,768]{2,1,0:T(8,128)(2,1)} %get-tuple-element.551.refs_1_, bf16[4,208,768]{2,1,0:T(8,128)(2,1)} %collective-permute-done.64.refs_2_), custom_call_target="tpu_custom_call" | custom-call | bytes 10000000 | tf_op jit(solution)/shard_map/join_images/pallas_call | solution.py:570
  363.0 3.3 collective-permute-start.73
  374.9 3.4 collective-permute-start.77
  (268 shorter events, 165.3 us)
Async XLA Ops:
  0.6 22.5 %collective-permute-start.2 = (bf16[768,3072]{1,0:T(8,128)(2,1)}, bf16[768,3072]{1,0:T(8,128)(2,1)}, u32[]{:S(2)}, u32[]{:S(2)}) collective-permute-start(bf16[768,3072]{1,0:T(8,128)(2,1)} %bitcast.182), channel_id=1, source_target_pairs={{0,8},{8,0},{16,24},{24,16},{1,9},{9,1},{17,25},{25,17},{2,10},{10... | collective-permute-start | bytes 14155784 | tf_op jit(solution)/shard_map/ppermute | solution.py:630
  0.8 22.4 %collective-permute-start.3 = (bf16[3072,768]{1,0:T(8,128)(2,1)}, bf16[3072,768]{1,0:T(8,128)(2,1)}, u32[]{:S(2)}, u32[]{:S(2)}) collective-permute-start(bf16[3072,768]{1,0:T(8,128)(2,1)} %bitcast.184), channel_id=1, source_target_pairs={{8,0},{24,16},{9,1},{25,17},{10,2},{26,18},{11,3},{27,19},{12,4},{... | collective-permute-start | bytes 14155784 | tf_op jit(solution)/shard_map/ppermute | solution.py:630
  5.2 10.3 %collective-permute-start.1 = (f32[8,768]{1,0:T(8,128)}, f32[8,768]{1,0:T(8,128)S(1)}, u32[]{:S(2)}, u32[]{:S(2)}) collective-permute-start(f32[8,768]{1,0:T(8,128)} %bitcast.190), channel_id=1, source_target_pairs={{0,8},{8,0},{16,24},{24,16},{1,9},{9,1},{17,25},{25,17},{2,10},{10... | collective-permute-start | bytes 73736 | tf_op jit(solution)/shard_map/ppermute | solution.py:630
  6.0 11.0 %collective-permute-start = (f32[12,732]{1,0:T(8,128)S(1)}, f32[12,732]{1,0:T(8,128)S(1)}, u32[]{:S(2)}, u32[]{:S(2)}) collective-permute-start(f32[12,732]{1,0:T(8,128)S(1)} %bitcast.189), channel_id=1, source_target_pairs={{0,8},{16,24},{1,9},{17,25},{2,10},{18,26},{3,11},{19,27},{4,12},{... | collective-permute-start | bytes 105416 | tf_op jit(solution)/shard_map/ppermute | solution.py:630
  34.8 36.8 %collective-permute-start.7 = (bf16[208,768]{1,0:T(8,128)(2,1)S(1)}, bf16[208,768]{1,0:T(8,128)(2,1)S(1)}, u32[]{:S(2)}, u32[]{:S(2)}) collective-permute-start(bf16[208,768]{1,0:T(8,128)(2,1)S(1)} %get-tuple-element.338), channel_id=1, source_target_pairs={{0,16},{8,24},{1,17},{9,25},{2,18},{10,26},{3,19},{11,27},{4,20},{... | collective-permute-start | bytes 958472 | tf_op jit(solution)/shard_map/ppermute | solution.py:630
  46.9 26.5 %collective-permute-start.6 = (bf16[208,768]{1,0:T(8,128)(2,1)S(1)}, bf16[208,768]{1,0:T(8,128)(2,1)S(1)}, u32[]{:S(2)}, u32[]{:S(2)}) collective-permute-start(bf16[208,768]{1,0:T(8,128)(2,1)S(1)} %get-tuple-element.337), channel_id=1, source_target_pairs={{0,16},{8,24},{1,17},{9,25},{2,18},{10,26},{3,19},{11,27},{4,20},{... | collective-permute-start | bytes 958472 | tf_op jit(solution)/shard_map/ppermute | solution.py:630
  58.6 19.8 %collective-permute-start.5 = (bf16[208,768]{1,0:T(8,128)(2,1)S(1)}, bf16[208,768]{1,0:T(8,128)(2,1)S(1)}, u32[]{:S(2)}, u32[]{:S(2)}) collective-permute-start(bf16[208,768]{1,0:T(8,128)(2,1)S(1)} %get-tuple-element.336), channel_id=1, source_target_pairs={{0,16},{8,24},{1,17},{9,25},{2,18},{10,26},{3,19},{11,27},{4,20},{... | collective-permute-start | bytes 958472 | tf_op jit(solution)/shard_map/ppermute | solution.py:630
  70.4 13.2 %collective-permute-start.4 = (bf16[208,768]{1,0:T(8,128)(2,1)S(1)}, bf16[208,768]{1,0:T(8,128)(2,1)S(1)}, u32[]{:S(2)}, u32[]{:S(2)}) collective-permute-start(bf16[208,768]{1,0:T(8,128)(2,1)S(1)} %get-tuple-element.335), channel_id=1, source_target_pairs={{0,16},{8,24},{1,17},{9,25},{2,18},{10,26},{3,19},{11,27},{4,20},{... | collective-permute-start | bytes 958472 | tf_op jit(solution)/shard_map/ppermute | solution.py:630
  93.2 22.4 %collective-permute-start.11 = (bf16[208,768]{1,0:T(8,128)(2,1)S(1)}, bf16[208,768]{1,0:T(8,128)(2,1)S(1)}, u32[]{:S(2)}, u32[]{:S(2)}) collective-permute-start(bf16[208,768]{1,0:T(8,128)(2,1)S(1)} %get-tuple-element.419), channel_id=1, source_target_pairs={{16,0},{24,8},{17,1},{25,9},{18,2},{26,10},{19,3},{27,11},{20,4},{... | collective-permute-start | bytes 958472 | tf_op jit(solution)/shard_map/ppermute | solution.py:630
  98.6 30.5 %collective-permute-start.10 = (bf16[208,768]{1,0:T(8,128)(2,1)S(1)}, bf16[208,768]{1,0:T(8,128)(2,1)S(1)}, u32[]{:S(2)}, u32[]{:S(2)}) collective-permute-start(bf16[208,768]{1,0:T(8,128)(2,1)S(1)} %get-tuple-element.418), channel_id=1, source_target_pairs={{16,0},{24,8},{17,1},{25,9},{18,2},{26,10},{19,3},{27,11},{20,4},{... | collective-permute-start | bytes 958472 | tf_op jit(solution)/shard_map/ppermute | solution.py:630
  104.1 38.6 %collective-permute-start.9 = (bf16[208,768]{1,0:T(8,128)(2,1)S(1)}, bf16[208,768]{1,0:T(8,128)(2,1)S(1)}, u32[]{:S(2)}, u32[]{:S(2)}) collective-permute-start(bf16[208,768]{1,0:T(8,128)(2,1)S(1)} %get-tuple-element.417), channel_id=1, source_target_pairs={{16,0},{24,8},{17,1},{25,9},{18,2},{26,10},{19,3},{27,11},{20,4},{... | collective-permute-start | bytes 958472 | tf_op jit(solution)/shard_map/ppermute | solution.py:630
  109.9 46.7 %collective-permute-start.8 = (bf16[208,768]{1,0:T(8,128)(2,1)S(1)}, bf16[208,768]{1,0:T(8,128)(2,1)S(1)}, u32[]{:S(2)}, u32[]{:S(2)}) collective-permute-start(bf16[208,768]{1,0:T(8,128)(2,1)S(1)} %get-tuple-element.416), channel_id=1, source_target_pairs={{16,0},{24,8},{17,1},{25,9},{18,2},{26,10},{19,3},{27,11},{20,4},{... | collective-permute-start | bytes 958472 | tf_op jit(solution)/shard_map/ppermute | solution.py:630
  192.4 10.6 %collective-permute-start.36 = (bf16[8,144,768]{2,1,0:T(8,128)(2,1)}, bf16[8,144,768]{2,1,0:T(8,128)(2,1)S(1)}, u32[]{:S(2)}, u32[]{:S(2)}) collective-permute-start(bf16[8,144,768]{2,1,0:T(8,128)(2,1)} %get-tuple-element.481), channel_id=1, source_target_pairs={{0,8},{8,0},{16,24},{24,16},{1,9},{9,1},{17,25},{25,17},{2,10},{10... | collective-permute-start | bytes 5308424 | tf_op jit(solution)/shard_map/ppermute | solution.py:630
  221.5 9.7 %collective-permute-start.39 = (bf16[144,768]{1,0:T(8,128)(2,1)S(1)}, bf16[144,768]{1,0:T(8,128)(2,1)S(1)}, u32[]{:S(2)}, u32[]{:S(2)}) collective-permute-start(bf16[144,768]{1,0:T(8,128)(2,1)S(1)} %fusion.1), channel_id=1, source_target_pairs={{0,1},{2,0},{4,2},{6,4},{7,6},{5,7},{3,5},{1,3},{8,9},{10,8},{12,1... | collective-permute-start | bytes 663560 | tf_op jit(solution)/shard_map/ppermute | solution.py:684
  278.4 32.5 %collective-permute-start.54 = (bf16[4,208,768]{2,1,0:T(8,128)(2,1)}, bf16[4,208,768]{2,1,0:T(8,128)(2,1)}, u32[]{:S(2)}, u32[]{:S(2)}) collective-permute-start(bf16[4,208,768]{2,1,0:T(8,128)(2,1)} %get-tuple-element.511), channel_id=1, source_target_pairs={{0,8},{8,0},{16,24},{24,16},{1,9},{9,1},{17,25},{25,17},{2,10},{10... | collective-permute-start | bytes 3833864 | tf_op jit(solution)/shard_map/ppermute | solution.py:630
  278.6 11.1 %collective-permute-start.46 = (bf16[2,96,768]{2,1,0:T(8,128)(2,1)S(1)}, bf16[2,96,768]{2,1,0:T(8,128)(2,1)S(1)}, u32[]{:S(2)}, u32[]{:S(2)}) collective-permute-start(bf16[2,96,768]{2,1,0:T(8,128)(2,1)S(1)} %get-tuple-element.489.refs_2_), channel_id=1, source_target_pairs={{0,1},{2,0},{4,2},{6,4},{7,6},{5,7},{3,5},{1,3},{8,9},{10,8},{12,1... | collective-permute-start | bytes 884744 | tf_op jit(solution)/shard_map/ppermute | solution.py:697
  279.8 9.9 %collective-permute-start.47 = (bf16[2,96,768]{2,1,0:T(8,128)(2,1)S(1)}, bf16[2,96,768]{2,1,0:T(8,128)(2,1)S(1)}, u32[]{:S(2)}, u32[]{:S(2)}) collective-permute-start(bf16[2,96,768]{2,1,0:T(8,128)(2,1)S(1)} %get-tuple-element.490.refs_1_), channel_id=1, source_target_pairs={{0,2},{2,4},{4,6},{6,7},{7,5},{5,3},{3,1},{1,0},{8,10},{10,12},{12... | collective-permute-start | bytes 884744 | tf_op jit(solution)/shard_map/ppermute | solution.py:697
  280.1 10.4 %collective-permute-start.48 = (bf16[2,96,768]{2,1,0:T(8,128)(2,1)S(1)}, bf16[2,96,768]{2,1,0:T(8,128)(2,1)S(1)}, u32[]{:S(2)}, u32[]{:S(2)}) collective-permute-start(bf16[2,96,768]{2,1,0:T(8,128)(2,1)S(1)} %get-tuple-element.491.refs_4_), channel_id=1, source_target_pairs={{8,9},{10,8},{12,10},{14,12},{15,14},{13,15},{11,13},{9,11},{24,25... | collective-permute-start | bytes 884744 | tf_op jit(solution)/shard_map/ppermute | solution.py:698
  311.0 29.6 %collective-permute-start.64 = (bf16[4,208,768]{2,1,0:T(8,128)(2,1)}, bf16[4,208,768]{2,1,0:T(8,128)(2,1)}, u32[]{:S(2)}, u32[]{:S(2)}) collective-permute-start(bf16[4,208,768]{2,1,0:T(8,128)(2,1)} %get-tuple-element.537), channel_id=1, source_target_pairs={{0,8},{8,0},{16,24},{24,16},{1,9},{9,1},{17,25},{25,17},{2,10},{10... | collective-permute-start | bytes 3833864 | tf_op jit(solution)/shard_map/ppermute | solution.py:630
  311.6 14.4 %collective-permute-start.55 = (bf16[2,96,768]{2,1,0:T(8,128)(2,1)S(1)}, bf16[2,96,768]{2,1,0:T(8,128)(2,1)S(1)}, u32[]{:S(2)}, u32[]{:S(2)}) collective-permute-start(bf16[2,96,768]{2,1,0:T(8,128)(2,1)S(1)} %collective-permute-done.50.refs_2_), channel_id=1, source_target_pairs={{0,1},{2,0},{4,2},{6,4},{7,6},{5,7},{3,5},{1,3},{8,9},{10,8},{12,1... | collective-permute-start | bytes 884744 | tf_op jit(solution)/shard_map/ppermute | solution.py:697
  312.9 13.1 %collective-permute-start.56 = (bf16[2,96,768]{2,1,0:T(8,128)(2,1)S(1)}, bf16[2,96,768]{2,1,0:T(8,128)(2,1)S(1)}, u32[]{:S(2)}, u32[]{:S(2)}) collective-permute-start(bf16[2,96,768]{2,1,0:T(8,128)(2,1)S(1)} %collective-permute-done.51.refs_1_), channel_id=1, source_target_pairs={{0,2},{2,4},{4,6},{6,7},{7,5},{5,3},{3,1},{1,0},{8,10},{10,12},{12... | collective-permute-start | bytes 884744 | tf_op jit(solution)/shard_map/ppermute | solution.py:697
  313.0 13.0 %collective-permute-start.57 = (bf16[2,96,768]{2,1,0:T(8,128)(2,1)S(1)}, bf16[2,96,768]{2,1,0:T(8,128)(2,1)S(1)}, u32[]{:S(2)}, u32[]{:S(2)}) collective-permute-start(bf16[2,96,768]{2,1,0:T(8,128)(2,1)S(1)} %collective-permute-done.52.refs_4_), channel_id=1, source_target_pairs={{8,9},{10,8},{12,10},{14,12},{15,14},{13,15},{11,13},{9,11},{24,25... | collective-permute-start | bytes 884744 | tf_op jit(solution)/shard_map/ppermute | solution.py:698
  316.3 9.8 %collective-permute-start.58 = (bf16[2,96,768]{2,1,0:T(8,128)(2,1)S(1)}, bf16[2,96,768]{2,1,0:T(8,128)(2,1)S(1)}, u32[]{:S(2)}, u32[]{:S(2)}) collective-permute-start(bf16[2,96,768]{2,1,0:T(8,128)(2,1)S(1)} %collective-permute-done.53.refs_3_), channel_id=1, source_target_pairs={{8,10},{10,12},{12,14},{14,15},{15,13},{13,11},{11,9},{9,8},{24,26... | collective-permute-start | bytes 884744 | tf_op jit(solution)/shard_map/ppermute | solution.py:698
  330.7 9.8 %collective-permute-start.63 = (bf16[2,96,768]{2,1,0:T(8,128)(2,1)S(1)}, bf16[2,96,768]{2,1,0:T(8,128)(2,1)S(1)}, u32[]{:S(2)}, u32[]{:S(2)}) collective-permute-start(bf16[2,96,768]{2,1,0:T(8,128)(2,1)S(1)} %collective-permute-done.58.refs_3_), channel_id=1, source_target_pairs={{8,10},{10,12},{12,14},{14,15},{15,13},{13,11},{11,9},{9,8},{24,26... | collective-permute-start | bytes 884744 | tf_op jit(solution)/shard_map/ppermute | solution.py:698
  340.6 18.9 %collective-permute-start.65 = (bf16[2,96,768]{2,1,0:T(8,128)(2,1)S(1)}, bf16[2,96,768]{2,1,0:T(8,128)(2,1)S(1)}, u32[]{:S(2)}, u32[]{:S(2)}) collective-permute-start(bf16[2,96,768]{2,1,0:T(8,128)(2,1)S(1)} %collective-permute-done.60.refs_2_), channel_id=1, source_target_pairs={{0,1},{2,0},{4,2},{6,4},{7,6},{5,7},{3,5},{1,3},{8,9},{10,8},{12,1... | collective-permute-start | bytes 884744 | tf_op jit(solution)/shard_map/ppermute | solution.py:697
  342.9 16.6 %collective-permute-start.66 = (bf16[2,96,768]{2,1,0:T(8,128)(2,1)S(1)}, bf16[2,96,768]{2,1,0:T(8,128)(2,1)S(1)}, u32[]{:S(2)}, u32[]{:S(2)}) collective-permute-start(bf16[2,96,768]{2,1,0:T(8,128)(2,1)S(1)} %collective-permute-done.61.refs_1_), channel_id=1, source_target_pairs={{0,2},{2,4},{4,6},{6,7},{7,5},{5,3},{3,1},{1,0},{8,10},{10,12},{12... | collective-permute-start | bytes 884744 | tf_op jit(solution)/shard_map/ppermute | solution.py:697
  342.9 16.6 %collective-permute-start.67 = (bf16[2,96,768]{2,1,0:T(8,128)(2,1)S(1)}, bf16[2,96,768]{2,1,0:T(8,128)(2,1)S(1)}, u32[]{:S(2)}, u32[]{:S(2)}) collective-permute-start(bf16[2,96,768]{2,1,0:T(8,128)(2,1)S(1)} %collective-permute-done.62.refs_4_), channel_id=1, source_target_pairs={{8,9},{10,8},{12,10},{14,12},{15,14},{13,15},{11,13},{9,11},{24,25... | collective-permute-start | bytes 884744 | tf_op jit(solution)/shard_map/ppermute | solution.py:698
  346.3 13.2 %collective-permute-start.68 = (bf16[2,96,768]{2,1,0:T(8,128)(2,1)S(1)}, bf16[2,96,768]{2,1,0:T(8,128)(2,1)S(1)}, u32[]{:S(2)}, u32[]{:S(2)}) collective-permute-start(bf16[2,96,768]{2,1,0:T(8,128)(2,1)S(1)} %collective-permute-done.63.refs_3_), channel_id=1, source_target_pairs={{8,10},{10,12},{12,14},{14,15},{15,13},{13,11},{11,9},{9,8},{24,26... | collective-permute-start | bytes 884744 | tf_op jit(solution)/shard_map/ppermute | solution.py:698
  370.8 15.6 %collective-permute-start.74 = (bf16[2,96,768]{2,1,0:T(8,128)(2,1)S(1)}, bf16[2,96,768]{2,1,0:T(8,128)(2,1)S(1)}, u32[]{:S(2)}, u32[]{:S(2)}) collective-permute-start(bf16[2,96,768]{2,1,0:T(8,128)(2,1)S(1)} %collective-permute-done.70.refs_2_), channel_id=1, source_target_pairs={{0,1},{2,0},{4,2},{6,4},{7,6},{5,7},{3,5},{1,3},{8,9},{10,8},{12,1... | collective-permute-start | bytes 884744 | tf_op jit(solution)/shard_map/ppermute | solution.py:697
  370.8 15.6 %collective-permute-start.75 = (bf16[2,96,768]{2,1,0:T(8,128)(2,1)S(1)}, bf16[2,96,768]{2,1,0:T(8,128)(2,1)S(1)}, u32[]{:S(2)}, u32[]{:S(2)}) collective-permute-start(bf16[2,96,768]{2,1,0:T(8,128)(2,1)S(1)} %collective-permute-done.71.refs_1_), channel_id=1, source_target_pairs={{0,2},{2,4},{4,6},{6,7},{7,5},{5,3},{3,1},{1,0},{8,10},{10,12},{12... | collective-permute-start | bytes 884744 | tf_op jit(solution)/shard_map/ppermute | solution.py:697
  373.0 13.4 %collective-permute-start.76 = (bf16[2,96,768]{2,1,0:T(8,128)(2,1)S(1)}, bf16[2,96,768]{2,1,0:T(8,128)(2,1)S(1)}, u32[]{:S(2)}, u32[]{:S(2)}) collective-permute-start(bf16[2,96,768]{2,1,0:T(8,128)(2,1)S(1)} %collective-permute-done.72.refs_4_), channel_id=1, source_target_pairs={{8,9},{10,8},{12,10},{14,12},{15,14},{13,15},{11,13},{9,11},{24,25... | collective-permute-start | bytes 884744 | tf_op jit(solution)/shard_map/ppermute | solution.py:698
  374.9 11.5 %collective-permute-start.77 = (bf16[2,96,768]{2,1,0:T(8,128)(2,1)S(1)}, bf16[2,96,768]{2,1,0:T(8,128)(2,1)S(1)}, u32[]{:S(2)}, u32[]{:S(2)}) collective-permute-start(bf16[2,96,768]{2,1,0:T(8,128)(2,1)S(1)} %collective-permute-done.73.refs_3_), channel_id=1, source_target_pairs={{8,10},{10,12},{12,14},{14,15},{15,13},{13,11},{11,9},{9,8},{24,26... | collective-permute-start | bytes 884744 | tf_op jit(solution)/shard_map/ppermute | solution.py:698
  (57 other events, 482.9 us)
